TPU v7x, 512 devices: a whole 4x8x8 slice. The times are simulated.
512 devices in a mesh: gx: 8 (over x, core), gy: 8 (over z), gz: 8 (over y).
Axes of the slice: x: 4, y: 8, z: 8, core: 2. Of those that a mesh axis runs over, the one named last changes fastest.
Arguments:
- positions: float32 [3, 32, 32, 6144], P(None, 'gx', 'gy', 'gz'), may hold values from 0 to 1
- charges: float32 [32, 32, 6144], P('gx', 'gy', 'gz'), may hold values from -0.625 to 0.625
- softening: float32 [32, 32, 6144], P('gx', 'gy', 'gz'), may hold values from 0.05 to 0.2
- counts: int32 [32, 32, 96], P('gx', 'gy', 'gz'), may hold values from 1 to 64
- top_locals: float32 [8, 8, 1536], P('gx', 'gy', 'gz'), may hold values from -6 to 6
- b_multipoles: bfloat16 [8, 8, 1536], P('gx', 'gy', 'gz'), may hold values from -24 to 24
- a_multipoles: bfloat16 [16, 16, 3072], P('gx', 'gy', 'gz'), may hold values from -12 to 12
- leaf_multipoles: bfloat16 [32, 32, 6144], P('gx', 'gy', 'gz'), may hold values from -6 to 6
- m2l_table: bfloat16 [343, 4096], replicated, may hold values from -0.0546875 to 0.0546875
- l2l_table: bfloat16 [8, 4096], replicated, may hold values from -0.75 to 0.75
Outputs:
- potential: float32 [32, 32, 6144], P('gx', 'gy', 'gz')
- leaf_locals: float32 [32, 32, 6144], P('gx', 'gy', 'gz')
Inputs may be any that keep to these rules, and one draw needn't show every extreme that they name: counts gives the live particles of each leaf; its slots at and beyond that number are padding.
All inputs are finite; a program needn't handle non-finite values.
Results may differ from a plain program's by a relative error of at most 0.008.
Values may be sent and summed in bfloat16 or wider, within the bound.
A program may use at most 128 MiB of HBM per device.

v0:
```python
import functools
import jax
import jax.numpy as jnp
from jax import lax
from jax.experimental import pallas as pl
from jax.experimental.pallas import tpu as pltpu
from jax.sharding import PartitionSpec as P

F32 = jnp.float32
BF16 = jnp.bfloat16
MESH = pl.DeviceIdType.MESH
AXES = ("gx", "gy", "gz")
T2_ROWS = 49 * 384 + 256


def iota(shape, dim):
    return lax.broadcasted_iota(jnp.int32, shape, dim)


def count_lanes(counts, pair):
    rows = counts.shape[0]
    lane = iota((rows, 128), 1)
    low = counts[:, 2 * pair : 2 * pair + 1]
    high = counts[:, 2 * pair + 1 : 2 * pair + 2]
    return jnp.where(lane < 64, low, high), lane & 63


def unpack_rows(block, base, s2, rows):
    for c in range(32):
        s2[pl.ds(base * 32 + c, rows, stride=32), :] = block[:, c * 128 : (c + 1) * 128]


def pair_rows(first, second, low_lanes):
    turned_first = pltpu.roll(first, 64, 1)
    turned_second = pltpu.roll(second, 64, 1)
    even = jnp.where(low_lanes, first, turned_second)
    odd = jnp.where(low_lanes, turned_first, second)
    return even.astype(BF16), odd.astype(BF16)


def exchange_kernel(
    pos, chg, soft, cnt, bm, am, lm, m2l_hbm, l2l,
    pf_out, ml_out, ma_out, mb_out, t2,
    pf, ml, ma, mb, zs, zr, ps, mls, mas, ms, zf, mt, s2,
    send, recv, local,
):
    gx, gy, gz = (lax.axis_index(a) for a in AXES)

    def at(ox, oy, oz):
        return (
            lax.rem(gx + (ox + 8), 8),
            lax.rem(gy + (oy + 8), 8),
            lax.rem(gz + (oz + 8), 8),
        )

    table = pltpu.make_async_copy(m2l_hbm, mt, local.at[0])
    table.start()
    barrier = pltpu.get_barrier_semaphore()
    around = [at(0, 0, 1), at(0, 0, -1)]
    for o in (1, -1, 2, -2, 3, -3):
        around += [at(o, 0, 0), at(0, o, 0)]
    for who in around:
        pl.semaphore_signal(barrier, inc=1, device_id=who, device_id_type=MESH)

    number = [0]

    def remote(src, dst, who):
        i = number[0]
        number[0] += 1
        copy = pltpu.make_async_remote_copy(
            src_ref=src, dst_ref=dst, send_sem=send.at[i], recv_sem=recv.at[i],
            device_id=who, device_id_type=MESH,
        )
        copy.start()
        return copy

    for x in range(4):
        block = lm[x].astype(F32)
        for zp in range(6):
            ms[zp * 16 + x * 4 : zp * 16 + x * 4 + 4, :] = block[:, zp * 128 : zp * 128 + 128]
    for x in range(2):
        block = am[x].astype(F32)
        for zp in range(3):
            ms[96 + zp * 4 + x * 2 : 98 + zp * 4 + x * 2, :] = block[:, zp * 128 : zp * 128 + 128]
    bcells = bm[0].astype(F32)
    ms[108:109, :] = bcells[:, 0:128]
    ms[109:110, :] = jnp.concatenate([bcells[:, 64:128], bcells[:, 128:192]], axis=1)
    ms[110:112, :] = jnp.zeros((2, 128), F32)
    row, col = iota((128, 128), 0), iota((128, 128), 1)
    moved = (row & 64) + ((row & 1) << 5) + ((row & 63) >> 1)
    order = jnp.where(moved == col, 1.0, 0.0).astype(BF16)
    ms[...] = jnp.dot(ms[...].astype(BF16), order, preferred_element_type=F32)

    ps[...] = jnp.zeros_like(ps)
    mas[...] = jnp.zeros_like(mas)
    zf[...] = jnp.zeros_like(zf)
    for x in range(4):
        fields = [pos[0, x] - 0.5, pos[1, x] - 0.5, pos[2, x] - 0.5, chg[x], soft[x]]
        counts = cnt[x]
        for zp in range(6):
            limit, slot = count_lanes(counts, zp)
            for f in range(5):
                piece = fields[f][:, zp * 128 : zp * 128 + 128]
                if f == 3:
                    piece = jnp.where(slot < limit, piece, 0.0)
                ps[pl.ds(x * 192 + f * 8 + 1 + zp, 4, stride=48), :] = piece
                if zp == 0:
                    zf[f * 16 + x * 4 : f * 16 + x * 4 + 4, :] = piece
                if zp == 5:
                    zf[112 + f * 16 + x * 4 : 112 + f * 16 + x * 4 + 4, :] = piece
    for side, (lp, ap) in enumerate(((0, 0), (5, 2))):
        base = side * 112
        zf[base + 80 : base + 96, :] = ms[lp * 16 : lp * 16 + 16, :]
        zf[base + 96 : base + 100, :] = ms[96 + ap * 4 : 100 + ap * 4, :]
        zf[base + 100 : base + 102, :] = ms[108:110, :]
        zs[side] = zf[base : base + 112, :].astype(BF16)
    pl.semaphore_wait(barrier, 14)

    z_copies = [
        remote(zs.at[0], zr.at[1], at(0, 0, -1)),
        remote(zs.at[1], zr.at[0], at(0, 0, 1)),
    ]
    for zp in range(6):
        for x in range(4):
            mls[pl.ds(x * 32 + zp + 1, 4, stride=8), :] = ms[
                zp * 16 + x * 4 : zp * 16 + x * 4 + 4, :
            ]
    for zp in range(3):
        for x in range(2):
            mas[pl.ds(x * 16 + zp + 1, 2, stride=8), :] = ms[
                96 + zp * 4 + x * 2 : 98 + zp * 4 + x * 2, :
            ]

    table.wait()

    def unpack(i, carry):
        block = mt[pl.ds(pl.multiple_of(i * 16, 16), 16), :].astype(F32)
        unpack_rows(block, i * 16, s2, 16)
        return carry

    lax.fori_loop(0, 21, unpack, 0)
    unpack_rows(mt[336:343, :].astype(F32), 336, s2, 7)
    unpack_rows(l2l[...].astype(F32), 343, s2, 8)

    for copy in z_copies:
        copy.wait()
    keep_low = jnp.where(gz > 0, 1.0, 0.0).astype(F32)
    keep_high = jnp.where(gz < 7, 1.0, 0.0).astype(F32)
    b_rows = []
    for side, (keep, zp_l, zp_a) in enumerate(((keep_low, 0, 0), (keep_high, 7, 4))):
        got = zr[side].astype(F32) * keep
        for x in range(4):
            for f in range(5):
                ps[pl.ds(x * 192 + f * 8 + zp_l, 4, stride=48), :] = got[
                    f * 16 + x * 4 : f * 16 + x * 4 + 4, :
                ]
            mls[pl.ds(x * 32 + zp_l, 4, stride=8), :] = got[80 + x * 4 : 84 + x * 4, :]
        for x in range(2):
            mas[pl.ds(x * 16 + zp_a, 2, stride=8), :] = got[96 + x * 2 : 98 + x * 2, :]
        b_rows.append((got[100:101, :], got[101:102, :]))
    (la, lb), (ra, rb) = b_rows
    oa, ob = ms[108:109, :], ms[109:110, :]
    low1 = iota((1, 128), 1) < 64
    middle = jnp.where(low1, pltpu.roll(lb, 64, 1), pltpu.roll(oa, 64, 1))
    middle_r = jnp.where(low1, pltpu.roll(ob, 64, 1), pltpu.roll(ra, 64, 1))
    pairs = [la, lb, middle, oa, ob, middle_r, ra, rb]
    even_z = lax.rem(gz, 2) == 0
    zf[0:16, :] = jnp.zeros((16, 128), F32)
    for l in range(3):
        at_even = l + 1 - l % 2
        at_odd = l + 1 - (l + 1) % 2
        for j in range(3):
            zf[4 * j + l : 4 * j + l + 1, :] = jnp.where(
                even_z, pairs[at_even + 2 * j], pairs[at_odd + 2 * j]
            )
    mb[3, 3] = zf[0:16, :].astype(BF16)
    x_b = []
    for o in (1, -1, 2, -2, 3, -3):
        x_b.append(remote(mb.at[3, 3], mb.at[3 - o, 3], at(o, 0, 0)))
    for x in range(4):
        for y in range(4):
            for t in range(3):
                r = (x * 4 + y) * 48 + t * 16
                pf[1 + x, 1 + y, t] = ps[r : r + 16, :].astype(BF16)
        for yp in range(2):
            r = x * 32 + yp * 16
            ml[2 + x, 1 + yp] = mls[r : r + 16, :].astype(BF16)
    for x in range(2):
        ma[2 + x, 1] = mas[x * 16 : x * 16 + 16, :].astype(BF16)

    own_x, own_xl, own_xa = pl.ds(1, 4), pl.ds(2, 4), pl.ds(2, 2)
    up, down = at(0, 1, 0), at(0, -1, 0)
    y_copies = [
        remote(pf.at[own_x, pl.ds(4, 1)], pf.at[own_x, pl.ds(0, 1)], up),
        remote(pf.at[own_x, pl.ds(1, 1)], pf.at[own_x, pl.ds(5, 1)], down),
        remote(ml.at[own_xl, pl.ds(2, 1)], ml.at[own_xl, pl.ds(0, 1)], up),
        remote(ml.at[own_xl, pl.ds(1, 1)], ml.at[own_xl, pl.ds(3, 1)], down),
        remote(ma.at[own_xa, pl.ds(1, 1)], ma.at[own_xa, pl.ds(0, 1)], up),
        remote(ma.at[own_xa, pl.ds(1, 1)], ma.at[own_xa, pl.ds(2, 1)], down),
    ]

    low_lanes = iota((32, 128), 1) < 64

    def pair_up(g, carry):
        near = (jnp.abs(g // 7 - 3) <= 1) & (jnp.abs(lax.rem(g, 7) - 3) <= 1)
        kept = jnp.where(near, 0.0, 1.0).astype(F32)
        tables = []
        for i in range(7):
            one = s2[pl.ds(pl.multiple_of((g * 7 + i) * 32, 32), 32), :]
            if 2 <= i <= 4:
                one = one * kept
            tables.append((one, pltpu.roll(one, 64, 1)))
        for w in range(6):
            (first, turned_first), (second, turned_second) = tables[w + 1], tables[w]
            to = g * 384 + w * 64
            t2[pl.ds(pl.multiple_of(to, 32), 32), :] = jnp.where(
                low_lanes, first, turned_second
            ).astype(BF16)
            t2[pl.ds(pl.multiple_of(to + 32, 32), 32), :] = jnp.where(
                low_lanes, turned_first, second
            ).astype(BF16)
        return carry

    lax.fori_loop(0, 20, pair_up, 0)
    for copy in x_b:
        copy.wait()
    y_b = []
    for o in (1, -1, 2, -2, 3, -3):
        y_b.append(remote(mb.at[:, pl.ds(3, 1)], mb.at[:, pl.ds(3 - o, 1)], at(0, o, 0)))
    for copy in y_copies:
        copy.wait()

    up, down = at(1, 0, 0), at(-1, 0, 0)
    x_copies = [
        remote(pf.at[pl.ds(4, 1)], pf.at[pl.ds(0, 1)], up),
        remote(pf.at[pl.ds(1, 1)], pf.at[pl.ds(5, 1)], down),
        remote(ml.at[pl.ds(4, 2)], ml.at[pl.ds(0, 2)], up),
        remote(ml.at[pl.ds(2, 2)], ml.at[pl.ds(6, 2)], down),
        remote(ma.at[pl.ds(2, 2)], ma.at[pl.ds(0, 2)], up),
        remote(ma.at[pl.ds(2, 2)], ma.at[pl.ds(4, 2)], down),
    ]
    lax.fori_loop(20, 49, pair_up, 0)
    for child in range(4):
        r = (343 + 2 * child) * 32
        even, odd = pair_rows(s2[r : r + 32, :], s2[r + 32 : r + 64, :], low_lanes)
        to = 49 * 384 + child * 64
        t2[to : to + 32, :] = even
        t2[to + 32 : to + 64, :] = odd
    for copy in x_copies + y_b:
        copy.wait()
    pf_out[...] = pf[...]
    ml_out[...] = ml[...]
    ma_out[...] = ma[...]
    mb_out[...] = mb[...]


def exchange(pos, chg, soft, cnt, bm, am, lm, m2l, l2l):
    vmem = pl.BlockSpec(memory_space=pltpu.VMEM)
    sizes = [(6, 6, 3, 16, 128), (8, 4, 16, 128), (6, 3, 16, 128), (7, 7, 16, 128)]
    return pl.pallas_call(
        exchange_kernel,
        name="exchange",
        out_shape=[jax.ShapeDtypeStruct(s, BF16) for s in sizes + [(T2_ROWS, 128)]],
        in_specs=[vmem] * 7 + [pl.BlockSpec(memory_space=pl.ANY), vmem],
        out_specs=[vmem] * 5,
        scratch_shapes=[pltpu.VMEM(s, BF16) for s in sizes]
        + [
            pltpu.VMEM((2, 112, 128), BF16),
            pltpu.VMEM((2, 112, 128), BF16),
            pltpu.VMEM((768, 128), F32),
            pltpu.VMEM((128, 128), F32),
            pltpu.VMEM((32, 128), F32),
            pltpu.VMEM((112, 128), F32),
            pltpu.VMEM((224, 128), F32),
            pltpu.VMEM((343, 4096), BF16),
            pltpu.VMEM((352 * 32, 128), F32),
            pltpu.SemaphoreType.DMA((26,)),
            pltpu.SemaphoreType.DMA((26,)),
            pltpu.SemaphoreType.DMA((1,)),
        ],
        compiler_params=pltpu.CompilerParams(
            collective_id=0, has_side_effects=True, vmem_limit_bytes=40 * 2**20
        ),
        cost_estimate=pl.CostEstimate(flops=10**7, bytes_accessed=10**7, transcendentals=0),
    )(pos, chg, soft, cnt, bm, am, lm, m2l, l2l)


def pieces(value, count):
    out = []
    for _ in range(count - 1):
        head = value.astype(BF16).astype(F32)
        out.append(head)
        value = value - head
    return out + [value]


def compute_kernel(
    gx, gy, gz,
    pf, ml, ma, mb, t2, pos, soft, cnt, top,
    pot_out, loc_out,
    a_mat, q_mat, b_mat, ft, fs, wt, near, lw, la, lb, lr, pa, ln,
):
    ones = jnp.ones((8, 128), F32)
    zp_row = iota((8, 128), 0)
    er, ec = iota((16, 1664), 0), iota((16, 1664), 1)
    leaf_of = jnp.where(ec < 768, (ec >> 6) + 2, ((ec - 768) >> 6) + 1)
    spread = jnp.where(((er & 7) * 2 + (er >> 3)) == leaf_of, 1.0, 0.0).astype(BF16)

    def column(c, slot):
        cx, cy = c // 6, lax.rem(c, 6)
        xy = pf[cx, cy, 0].astype(F32)
        zq = pf[cx, cy, 1].astype(F32)
        s = pf[cx, cy, 2].astype(F32)[0:8]
        x, y, z, q = xy[0:8], xy[8:16], zq[0:8], zq[8:16]
        out = ((cx == 0) & (gx == 0)) | ((cx == 5) & (gx == 7))
        out = out | ((cy == 0) & (gy == 0)) | ((cy == 5) & (gy == 7))
        q = q * jnp.where(out, 0.0, 1.0).astype(F32)
        fx, fy = cx.astype(F32) - 2.5, cy.astype(F32) - 2.5
        ix, iy = ones * fx, ones * fy
        n = (x + ix) * (x + ix) + (y + iy) * (y + iy) + z * z + 0.5 * (s * s)
        feats = [x, x, ix, ix, y, y, iy, iy, z, z, ones, ones, ones] + pieces(n, 3)
        for f in range(16):
            wt[slot, pl.ds(f, 8, stride=16), :] = feats[f]
        turned = wt[slot].T.astype(BF16)
        rows = pl.ds(pl.multiple_of(c * 64, 64), 64)
        a_mat[rows, 0:128] = turned[0:64]
        a_mat[rows, 128:256] = turned[64:128]
        qt = q.T
        qq = jnp.concatenate([qt[0:64], qt[64:128]], axis=1).astype(BF16)
        q_mat[rows, :] = jnp.dot(qq, spread, preferred_element_type=F32).astype(BF16)

    def columns(i, carry):
        for u in range(4):
            column(i * 4 + u, u)
        return carry

    lax.fori_loop(0, 9, columns, 0)

    lane = iota((64, 128), 1)

    def put(f, v):
        for zp in range(6):
            fs[zp, pl.ds(f, 4, stride=16), :] = v[:, zp * 128 : zp * 128 + 128]

    for x in range(4):
        px, py, pz = (pos[d, x] - 0.5 for d in range(3))
        s = soft[x]
        fx = px + (x - 1.5)
        fy = py + (iota((4, 768), 0).astype(F32) - 1.5)
        ax, bx = pieces(fx, 2)
        ay, by = pieces(fy, 2)
        bx, by = bx.astype(BF16).astype(F32), by.astype(BF16).astype(F32)
        xx, yy = ax + bx, ay + by
        base = xx * xx + yy * yy + 0.5 * (s * s)
        for f, v in ((0, ax), (1, bx), (2, ax), (3, bx), (4, ay), (5, by), (6, ay), (7, by)):
            put(f, -2.0 * v)
        for f in (13, 14, 15):
            put(f, jnp.ones((4, 768), F32))
        for d in range(3):
            az, bz = pieces(pz - (d - 1.0), 2)
            bz = bz.astype(BF16).astype(F32)
            zz = az + bz
            n = base + zz * zz
            for f, v in zip((8, 9, 10, 11, 12), [-2.0 * az, -2.0 * bz] + pieces(n, 3)):
                put(f, v)
            for zp in range(6):
                made = fs[zp]
                for e in range(2):
                    mine = lane < 64 if e == 0 else lane >= 64
                    half = jnp.where(mine, made, 0.0).astype(BF16)
                    for y in range(4):
                        ft[x * 4 + y, d, e, :, zp * 128 : zp * 128 + 128] = half[
                            y * 16 : y * 16 + 16
                        ]

    b_mat[...] = jnp.zeros_like(b_mat)
    other = jnp.where(iota((64, 256), 0) == (iota((64, 256), 1) & 63), 0.0, 1.0).astype(F32)
    other = jnp.concatenate([jnp.ones((64, 256), F32), other, jnp.ones((64, 256), F32)], axis=0)
    offsets = (768, 0, 896)

    def group(g, carry):
        x, y = g // 4, lax.rem(g, 4)
        for k in range(3):
            for d in range(3):
                for h in range(2):
                    for e in range(2):
                        cell = 4 * k + 2 + 2 * h + e + d - 1
                        r = (cell % 2) * 128 + (cell // 2) * 16
                        b_mat[k * 3 + d, r : r + 16, h * 128 : h * 128 + 128] = ft[
                            g, d, e, :, (2 * k + h) * 128 : (2 * k + h) * 128 + 128
                        ]
        for k in range(3):
            acc = jnp.zeros((8, 256), F32)
            for d in range(3):
                weights = b_mat[k * 3 + d]
                at_q = offsets[d] + 256 * k
                for dx in range(3):
                    rows = pl.ds(pl.multiple_of(((x + dx) * 6 + y) * 64, 64), 192)
                    r2 = jnp.dot(a_mat[rows, :], weights, preferred_element_type=F32)
                    q = q_mat[rows, at_q : at_q + 256].astype(F32)
                    if d == 1 and dx == 1:
                        q = q * other
                    acc = acc + jnp.sum((lax.rsqrt(r2) * q).reshape(24, 8, 256), axis=0)
            near[pl.ds(g, 1), k * 256 : k * 256 + 256] = jnp.sum(acc, axis=0, keepdims=True)
        return carry

    lax.fori_loop(0, 16, group, 0)

    def shifted(v):
        return [v, pltpu.roll(v, 7, 0), pltpu.roll(v, 6, 0)]

    def inside(coord, offset):
        return (coord + offset >= 0) & (coord + offset <= 7)

    for xs in range(8):
        over_x = -1 if xs < 2 else (1 if xs >= 6 else 0)
        turned = []
        for yp in range(4):
            over_y = -1 if yp < 1 else (1 if yp >= 3 else 0)
            keep = jnp.where(inside(gx, over_x) & inside(gy, over_y), 1.0, 0.0).astype(F32)
            tile = ml[xs, yp].astype(F32) * keep
            turned.append((shifted(tile[0:8]), shifted(tile[8:16])))
        for w in range(6):
            for j in range(3):
                lw[xs, w, :, j * 128 : j * 128 + 128] = jnp.concatenate(
                    [turned[w // 2][w % 2][j], turned[w // 2 + 1][w % 2][j]], axis=0
                ).astype(BF16)
    zero8 = jnp.zeros((8, 128), F32)
    a_tiles = {}
    for xs in range(6):
        over_x = -1 if xs < 2 else (1 if xs >= 4 else 0)
        for yp in range(3):
            over_y = yp - 1
            keep = jnp.where(inside(gx, over_x) & inside(gy, over_y), 1.0, 0.0).astype(F32)
            tile = ma[xs, yp].astype(F32) * keep
            a_tiles[xs, yp] = (shifted(tile[0:8]), shifted(tile[8:16]))
    for dx in range(7):
        for w in range(6):
            for j in range(3):
                first = a_tiles[dx - 1, w // 2][w % 2][j] if dx >= 1 else zero8
                second = a_tiles[dx, w // 2][w % 2][j] if dx <= 5 else zero8
                la[dx, w, :, j * 128 : j * 128 + 128] = jnp.concatenate(
                    [first, second], axis=0
                ).astype(BF16)
    row16 = iota((16, 128), 0)
    odd_x, odd_y = lax.rem(gx, 2), lax.rem(gy, 2)
    for dx in range(7):
        ok_x = inside(gx, dx - 3)
        if dx == 0:
            ok_x = ok_x & (odd_x == 1)
        if dx == 6:
            ok_x = ok_x & (odd_x == 0)
        for w in range(6):
            dy = w + 1 - odd_y
            keep = jnp.where(ok_x & inside(gy, dy - 3), 1.0, 0.0).astype(F32)
            tile = mb[dx, dy].astype(F32) * keep
            for j in range(3):
                lb[dx, w, :, j * 128 : j * 128 + 128] = jnp.where(
                    (row16 >> 2) == j, tile, 0.0
                ).astype(BF16)

    total = [jnp.zeros((16, 256), F32) for _ in range(6)]
    for dx in range(7):
        xs_of = [x for x in range(4) if not (dx == 0 and x % 2 == 0) and not (dx == 6 and x % 2 == 1)]
        for w in range(6):
            g = dx * 7 + w + 1
            weights = jnp.concatenate(
                [t2[g * 384 : (g + 1) * 384, :], t2[(g - 1) * 384 : g * 384, :]], axis=1
            )
            left = [lw[x + dx - 1, w] for x in xs_of] + [la[dx, w], lb[dx, w]]
            made = jnp.dot(
                jnp.concatenate(left, axis=0), weights, preferred_element_type=F32
            )
            for i, slot in enumerate(xs_of + [4, 5]):
                total[slot] = total[slot] + made[i * 16 : i * 16 + 16]

    row, col = iota((64, 64), 0), iota((64, 64), 1)
    order = jnp.where(((row & 1) << 5) + (row >> 1) == col, 1.0, 0.0).astype(BF16)

    def ordered(v):
        return jnp.dot(v.astype(BF16), order, preferred_element_type=F32).astype(BF16)

    v_of = []
    for px in range(2):
        r = 49 * 384 + px * 128
        v_of.append(jnp.concatenate([t2[r : r + 64, :], t2[r + 64 : r + 128, :]], axis=1))
    sb = total[5]
    sb = sb[0:4] + sb[4:8] + sb[8:12]
    sb = jnp.where(odd_y == 1, sb[:, 128:256], sb[:, 0:128])
    parity = lax.rem(iota((4, 64), 0) + gz, 2)
    sb = jnp.where(parity == 1, sb[:, 64:128], sb[:, 0:64])
    topv = top[0]
    top4 = jnp.concatenate(
        [topv[:, 0:64], topv[:, 64:128], topv[:, 128:192], jnp.zeros((1, 64), F32)], axis=0
    )
    local_b = ordered(jnp.concatenate([top4 + 0.25 * sb, jnp.zeros((12, 64), F32)], axis=0))
    for xa in range(2):
        down = jnp.dot(local_b, v_of[xa], preferred_element_type=F32)[0:4]
        local_a = 0.5 * total[4][xa * 8 : xa * 8 + 4] + down
        for ya in range(2):
            for p in range(2):
                b = ya * 128 + p * 64
                pa[pl.ds(xa * 16 + ya * 8 + p, 4, stride=2), 0:64] = local_a[:, b : b + 64]
    for xa in range(2):
        parent = ordered(pa[xa * 16 : xa * 16 + 16, 0:64])
        for px in range(2):
            x = 2 * xa + px
            leaf = total[x] + jnp.dot(parent, v_of[px], preferred_element_type=F32)
            lr[x * 32 : x * 32 + 16, :] = leaf[:, 0:128]
            lr[x * 32 + 16 : x * 32 + 32, :] = leaf[:, 128:256]
    for x in range(4):
        for y in range(4):
            for zp in range(6):
                r = x * 32 + (y % 2) * 16 + (y // 2) * 8 + zp
                ln[x * 4 + y : x * 4 + y + 1, zp * 128 : zp * 128 + 128] = lr[r : r + 1, :]

    lane8 = iota((8, 128), 1)
    for i in range(2):
        for zp in range(6):
            lanes = slice(zp * 128, zp * 128 + 128)
            coef = ln[i * 8 : i * 8 + 8, lanes]
            cheb = []
            for d in range(3):
                u = 2.0 * jnp.concatenate(
                    [pos[d, 2 * i, :, lanes], pos[d, 2 * i + 1, :, lanes]], axis=0
                ) - 1.0
                t2nd = 2.0 * u * u - 1.0
                cheb.append([None, u, t2nd, 2.0 * u * t2nd - u])
            out = None
            for a in range(4):
                sum_b = None
                for b in range(4):
                    sum_c = None
                    for c in range(4):
                        index = (lane8 & 64) + (16 * a + 4 * b + c)
                        term = jnp.take_along_axis(coef, index, axis=1, mode="promise_in_bounds")
                        if c:
                            term = term * cheb[2][c]
                        sum_c = term if sum_c is None else sum_c + term
                    if b:
                        sum_c = sum_c * cheb[1][b]
                    sum_b = sum_c if sum_b is None else sum_b + sum_c
                if a:
                    sum_b = sum_b * cheb[0][a]
                out = sum_b if out is None else out + sum_b
            value = out * 0.125 + near[i * 8 : i * 8 + 8, lanes]
            limit, slot = count_lanes(
                jnp.concatenate([cnt[2 * i], cnt[2 * i + 1]], axis=0), zp
            )
            value = jnp.where(slot < limit, value, 0.0)
            for h in range(2):
                pot_out[2 * i + h, :, lanes] = value[h * 4 : h * 4 + 4]
                loc_out[2 * i + h, :, lanes] = coef[h * 4 : h * 4 + 4]


def compute_entry(*refs):
    compute_kernel(*(lax.axis_index(a) for a in AXES), *refs)


def compute(pf, ml, ma, mb, t2, pos, soft, cnt, top, body=compute_entry):
    vmem = pl.BlockSpec(memory_space=pltpu.VMEM)
    return pl.pallas_call(
        body,
        name="compute",
        out_shape=[jax.ShapeDtypeStruct((4, 4, 768), F32)] * 2,
        in_specs=[vmem] * 9,
        out_specs=[vmem] * 2,
        scratch_shapes=[
            pltpu.VMEM((2304, 256), BF16),
            pltpu.VMEM((2304, 1664), BF16),
            pltpu.VMEM((9, 256, 256), BF16),
            pltpu.VMEM((16, 3, 2, 16, 768), BF16),
            pltpu.VMEM((6, 64, 128), F32),
            pltpu.VMEM((4, 128, 128), F32),
            pltpu.VMEM((16, 768), F32),
            pltpu.VMEM((8, 6, 16, 384), BF16),
            pltpu.VMEM((7, 6, 16, 384), BF16),
            pltpu.VMEM((7, 6, 16, 384), BF16),
            pltpu.VMEM((128, 128), F32),
            pltpu.VMEM((32, 128), F32),
            pltpu.VMEM((16, 768), F32),
        ],
        compiler_params=pltpu.CompilerParams(vmem_limit_bytes=48 * 2**20),
        cost_estimate=pl.CostEstimate(flops=10**10, bytes_accessed=10**7, transcendentals=2 * 10**7),
    )(pf, ml, ma, mb, t2, pos, soft, cnt, top)


def per_device(pos, chg, soft, cnt, top, bm, am, lm, m2l, l2l):
    halos = exchange(pos, chg, soft, cnt, bm, am, lm, m2l, l2l)
    return tuple(compute(*halos, pos, soft, cnt, top))


def solution(mesh):
    split = P("gx", "gy", "gz")
    in_specs = (P(None, "gx", "gy", "gz"),) + (split,) * 7 + (P(), P())
    return jax.shard_map(
        per_device, mesh=mesh, in_specs=in_specs, out_specs=(split, split), check_vma=False
    )
```

profile of v0, /device:TPU:1, one launch (start us, length us, event | category | flops | bytes accessed | tf_op | source)
XLA Modules:
  0.0 67.1 jit_solution(11120891039581545540)
XLA Ops:
  0.6 0.0 copy-start
  0.6 1.8 %copy-done = bf16[343,4096]{1,0:T(8,128)(2,1)S(1)} copy-done((bf16[343,4096]{1,0:T(8,128)(2,1)S(1)}, bf16[343,4096]{1,0:T(8,128)(2,1)}, u32[]{:S(2)}) %copy-start) | copy-done | bytes 2809880
  2.4 0.9 %copy-done.1 = f32[3,4,4,768]{3,2,1,0:T(4,128)S(1)} copy-done((f32[3,4,4,768]{3,2,1,0:T(4,128)S(1)}, f32[3,4,4,768]{3,2,1,0:T(4,128)}, u32[]{:S(2)}) %copy-start.1) | copy-done | bytes 147480
  3.3 0.0 copy-start.3
  3.3 0.8 %copy-done.3 = bf16[8,4096]{1,0:T(8,128)(2,1)S(1)} copy-done((bf16[8,4096]{1,0:T(8,128)(2,1)S(1)}, bf16[8,4096]{1,0:T(8,128)(2,1)}, u32[]{:S(2)}) %copy-start.3) | copy-done | bytes 65560
  4.2 0.0 copy-start.4
  4.2 0.8 %copy-done.4 = f32[4,4,768]{2,1,0:T(4,128)S(1)} copy-done((f32[4,4,768]{2,1,0:T(4,128)S(1)}, f32[4,4,768]{2,1,0:T(4,128)}, u32[]{:S(2)}) %copy-start.4) | copy-done | bytes 49176
  5.0 0.0 copy-start.5
  5.0 0.8 %copy-done.5 = f32[4,4,768]{2,1,0:T(4,128)S(1)} copy-done((f32[4,4,768]{2,1,0:T(4,128)S(1)}, f32[4,4,768]{2,1,0:T(4,128)}, u32[]{:S(2)}) %copy-start.5) | copy-done | bytes 49176
  5.8 0.0 copy-start.7
  5.8 0.7 %copy-done.7 = bf16[4,4,768]{2,1,0:T(4,128)(2,1)S(1)} copy-done((bf16[4,4,768]{2,1,0:T(4,128)(2,1)S(1)}, bf16[4,4,768]{2,1,0:T(4,128)(2,1)}, u32[]{:S(2)}) %copy-start.7) | copy-done | bytes 24600
  6.5 0.0 copy-start.8
  6.5 0.7 %copy-done.8 = s32[4,4,12]{2,1,0:T(4,128)S(1)} copy-done((s32[4,4,12]{2,1,0:T(4,128)S(1)}, s32[4,4,12]{2,1,0:T(4,128)}, u32[]{:S(2)}) %copy-start.8) | copy-done | bytes 792
  7.2 0.0 copy-start.10
  7.2 0.7 %copy-done.10 = bf16[2,2,384]{2,1,0:T(2,128)(2,1)S(1)} copy-done((bf16[2,2,384]{2,1,0:T(2,128)(2,1)S(1)}, bf16[2,2,384]{2,1,0:T(2,128)(2,1)}, u32[]{:S(2)}) %copy-start.10) | copy-done | bytes 3096
  7.9 0.0 copy-start.11
  7.9 0.7 %copy-done.11 = bf16[1,1,192]{2,1,0:T(2,128)(2,1)S(1)} copy-done((bf16[1,1,192]{2,1,0:T(2,128)(2,1)S(1)}, bf16[1,1,192]{2,1,0:T(2,128)(2,1)}, u32[]{:S(2)}) %copy-start.11) | copy-done | bytes 408
  8.6 27.4 %exchange.1 = (bf16[6,6,3,16,128]{4,3,2,1,0:T(8,128)(2,1)S(1)}, bf16[8,4,16,128]{3,2,1,0:T(8,128)(2,1)S(1)}, bf16[6,3,16,128]{3,2,1,0:T(8,128)(2,1)S(1)}, bf16[7...) custom-call(f32[3,4,4,768]{3,2,1,0:T(4,128)S(1)} %copy-done.1, f32[4,4,768]{2,1,0:T(4,128)S(1)} %copy-done.4, ...), custom_call_target="tpu_custom_call" | custom-call | flops 10000000 | bytes 10000000 | tf_op jit(solution)/shard_map/exchange/pallas_call | solution.py:260
  36.0 0.0 copy-start.2
  36.0 0.9 %copy-done.2 = f32[3,4,4,768]{3,2,1,0:T(4,128)S(1)} copy-done((f32[3,4,4,768]{3,2,1,0:T(4,128)S(1)}, f32[3,4,4,768]{3,2,1,0:T(4,128)}, u32[]{:S(2)}) %copy-start.2) | copy-done | bytes 147480
  36.9 0.8 %copy-done.6 = f32[4,4,768]{2,1,0:T(4,128)S(1)} copy-done((f32[4,4,768]{2,1,0:T(4,128)S(1)}, f32[4,4,768]{2,1,0:T(4,128)}, u32[]{:S(2)}) %copy-start.6) | copy-done | bytes 49176
  37.7 0.7 %copy-done.9 = s32[4,4,12]{2,1,0:T(4,128)S(1)} copy-done((s32[4,4,12]{2,1,0:T(4,128)S(1)}, s32[4,4,12]{2,1,0:T(4,128)}, u32[]{:S(2)}) %copy-start.9) | copy-done | bytes 792
  38.4 0.7 %copy-done.12 = f32[1,1,192]{2,1,0:T(1,128)S(1)} copy-done((f32[1,1,192]{2,1,0:T(1,128)S(1)}, f32[1,1,192]{2,1,0:T(1,128)}, u32[]{:S(2)}) %copy-start.12) | copy-done | bytes 792
  39.1 28.1 %compute.1 = (f32[4,4,768]{2,1,0:T(4,128)}, f32[4,4,768]{2,1,0:T(4,128)}) custom-call(bf16[6,6,3,16,128]{4,3,2,1,0:T(8,128)(2,1)S(1)} %get-tuple-element.7.refs_0_, bf16[8,4,16,128]{3,2,1,0:T(8,128)(2,1)S(1)} %get-tuple-element.8.refs_1_, bf16[6,3,16,128]{3,2,1,0:T(8,128)(2,1)S(1)} %get-tuple-element.9.refs_2_, ...), custom_call_target="tpu_custom_call" | custom-call | flops 10000000000 | bytes 10000000 | tf_op jit(solution)/shard_map/compute/pallas_call | solution.py:562
  (4 shorter events, 0.0 us)
Async XLA Ops:
  0.6 1.8 %copy-start = (bf16[343,4096]{1,0:T(8,128)(2,1)S(1)}, bf16[343,4096]{1,0:T(8,128)(2,1)}, u32[]{:S(2)}) copy-start(bf16[343,4096]{1,0:T(8,128)(2,1)} %m2l_hbm.1) | copy-start | bytes 8429572
  2.4 0.9 %copy-start.1 = (f32[3,4,4,768]{3,2,1,0:T(4,128)S(1)}, f32[3,4,4,768]{3,2,1,0:T(4,128)}, u32[]{:S(2)}) copy-start(f32[3,4,4,768]{3,2,1,0:T(4,128)} %refs_5_.1) | copy-start | bytes 442372
  3.3 0.8 %copy-start.3 = (bf16[8,4096]{1,0:T(8,128)(2,1)S(1)}, bf16[8,4096]{1,0:T(8,128)(2,1)}, u32[]{:S(2)}) copy-start(bf16[8,4096]{1,0:T(8,128)(2,1)} %l2l.1) | copy-start | bytes 196612
  4.2 0.8 %copy-start.4 = (f32[4,4,768]{2,1,0:T(4,128)S(1)}, f32[4,4,768]{2,1,0:T(4,128)}, u32[]{:S(2)}) copy-start(f32[4,4,768]{2,1,0:T(4,128)} %chg.1) | copy-start | bytes 147460
  5.0 0.8 %copy-start.5 = (f32[4,4,768]{2,1,0:T(4,128)S(1)}, f32[4,4,768]{2,1,0:T(4,128)}, u32[]{:S(2)}) copy-start(f32[4,4,768]{2,1,0:T(4,128)} %refs_6_.1) | copy-start | bytes 147460
  5.8 0.7 %copy-start.7 = (bf16[4,4,768]{2,1,0:T(4,128)(2,1)S(1)}, bf16[4,4,768]{2,1,0:T(4,128)(2,1)}, u32[]{:S(2)}) copy-start(bf16[4,4,768]{2,1,0:T(4,128)(2,1)} %lm.1) | copy-start | bytes 73732
  6.5 0.7 %copy-start.8 = (s32[4,4,12]{2,1,0:T(4,128)S(1)}, s32[4,4,12]{2,1,0:T(4,128)}, u32[]{:S(2)}) copy-start(s32[4,4,12]{2,1,0:T(4,128)} %refs_7_.1) | copy-start | bytes 2308
  7.2 0.7 %copy-start.10 = (bf16[2,2,384]{2,1,0:T(2,128)(2,1)S(1)}, bf16[2,2,384]{2,1,0:T(2,128)(2,1)}, u32[]{:S(2)}) copy-start(bf16[2,2,384]{2,1,0:T(2,128)(2,1)} %am.1) | copy-start | bytes 9220
  7.9 0.7 %copy-start.11 = (bf16[1,1,192]{2,1,0:T(2,128)(2,1)S(1)}, bf16[1,1,192]{2,1,0:T(2,128)(2,1)}, u32[]{:S(2)}) copy-start(bf16[1,1,192]{2,1,0:T(2,128)(2,1)} %bm.1) | copy-start | bytes 1156
  36.0 0.9 %copy-start.2 = (f32[3,4,4,768]{3,2,1,0:T(4,128)S(1)}, f32[3,4,4,768]{3,2,1,0:T(4,128)}, u32[]{:S(2)}) copy-start(f32[3,4,4,768]{3,2,1,0:T(4,128)} %refs_5_.1) | copy-start | bytes 442372
  36.9 0.8 %copy-start.6 = (f32[4,4,768]{2,1,0:T(4,128)S(1)}, f32[4,4,768]{2,1,0:T(4,128)}, u32[]{:S(2)}) copy-start(f32[4,4,768]{2,1,0:T(4,128)} %refs_6_.1) | copy-start | bytes 147460
  37.7 0.7 %copy-start.9 = (s32[4,4,12]{2,1,0:T(4,128)S(1)}, s32[4,4,12]{2,1,0:T(4,128)}, u32[]{:S(2)}) copy-start(s32[4,4,12]{2,1,0:T(4,128)} %refs_7_.1) | copy-start | bytes 2308
  38.4 0.7 %copy-start.12 = (f32[1,1,192]{2,1,0:T(1,128)S(1)}, f32[1,1,192]{2,1,0:T(1,128)}, u32[]{:S(2)}) copy-start(f32[1,1,192]{2,1,0:T(1,128)} %refs_8_.1) | copy-start | bytes 2308
where the time goes:
time: 67.8 us; the launch traced here: 67.1 us
  Pallas kernels  55.5 us (82%)
  local copies, waits for them, and re-layouts  11 us (16%)
    pallas_call x1, Pallas kernels, compute(): pl.pallas_call(body, name='compute', out_shape=[jax.ShapeDtypeStruct((4,...  28.1 us
    pallas_call x1, Pallas kernels, exchange(): pl.pallas_call(exchange_kernel, name='exchange', out_shape=[jax.ShapeDtyp...  27.4 us
    unnamed x26, local copies, waits for them, and re-layouts  11 us

commit v1 on v0

v1 whole, which is shorter than its diff:
```python
import functools
import jax
import jax.numpy as jnp
from jax import lax
from jax.experimental import pallas as pl
from jax.experimental.pallas import tpu as pltpu
from jax.sharding import PartitionSpec as P

F32 = jnp.float32
BF16 = jnp.bfloat16
MESH = pl.DeviceIdType.MESH
AXES = ("gx", "gy", "gz")
T2_ROWS = 49 * 384 + 256
VMEM_BYTES = 63 * 2**20


def iota(shape, dim):
    return lax.broadcasted_iota(jnp.int32, shape, dim)


def count_lanes(counts, pair):
    rows = counts.shape[0]
    lane = iota((rows, 128), 1)
    low = counts[:, 2 * pair : 2 * pair + 1]
    high = counts[:, 2 * pair + 1 : 2 * pair + 2]
    return jnp.where(lane < 64, low, high), lane & 63


def unpack_rows(block, base, s2, rows):
    for c in range(32):
        s2[pl.ds(base * 32 + c, rows, stride=32), :] = block[:, c * 128 : (c + 1) * 128]


def pair_rows(first, second, low_lanes):
    turned_first = pltpu.roll(first, 64, 1)
    turned_second = pltpu.roll(second, 64, 1)
    even = jnp.where(low_lanes, first, turned_second)
    odd = jnp.where(low_lanes, turned_first, second)
    return even.astype(BF16), odd.astype(BF16)


def pieces(value, count):
    out = []
    for _ in range(count - 1):
        head = value.astype(BF16).astype(F32)
        out.append(head)
        value = value - head
    return out + [value]


def inside(coord, offset):
    return (coord + offset >= 0) & (coord + offset <= 7)


def source_columns(where, gx, gy, pf, wt, a_mat, q_mat):
    ones = jnp.ones((8, 128), F32)
    same = jnp.where(iota((128, 128), 0) == iota((128, 128), 1), 1.0, 0.0).astype(BF16)
    er, ec = iota((16, 1024), 0), iota((16, 1024), 1)
    spread = jnp.where(((er & 7) * 2 + (er >> 3)) == (ec >> 6), 1.0, 0.0).astype(BF16)
    charges = []
    for slot, (cx, cy) in enumerate(where):
        xy = pf[cx, cy, 0].astype(F32)
        zq = pf[cx, cy, 1].astype(F32)
        s = pf[cx, cy, 2].astype(F32)[0:8]
        x, y, z, q = xy[0:8], xy[8:16], zq[0:8], zq[8:16]
        over_x = jnp.where(cx == 0, -1, jnp.where(cx == 5, 1, 0))
        over_y = jnp.where(cy == 0, -1, jnp.where(cy == 5, 1, 0))
        q = q * jnp.where(inside(gx, over_x) & inside(gy, over_y), 1.0, 0.0).astype(F32)
        ix = ones * (jnp.asarray(cx, F32) - 2.5)
        iy = ones * (jnp.asarray(cy, F32) - 2.5)
        n = (x + ix) * (x + ix) + (y + iy) * (y + iy) + z * z + 0.5 * (s * s)
        feats = [x, x, ix, ix, y, y, iy, iy, z, z, ones, ones, ones] + pieces(n, 3)
        for f in range(16):
            wt[slot, pl.ds(f, 8, stride=16), :] = feats[f]
        wt[slot, 128:136, :] = q
    for slot, (cx, cy) in enumerate(where):
        turned = lax.dot_general(
            same, wt[slot].astype(BF16), (((1,), (1,)), ((), ())), preferred_element_type=F32
        )
        rows = pl.ds(pl.multiple_of((cx * 6 + cy) * 64, 64), 64)
        a_mat[rows, 0:128] = turned[0:64, 0:128].astype(BF16)
        a_mat[rows, 128:256] = turned[64:128, 0:128].astype(BF16)
        charges.append(
            jnp.concatenate([turned[0:64, 128:136], turned[64:128, 128:136]], axis=1)
        )
    wide = jnp.dot(
        jnp.concatenate(charges, axis=0).astype(BF16), spread, preferred_element_type=F32
    )
    low = iota((64, 128), 1) < 64
    for slot, (cx, cy) in enumerate(where):
        rows = pl.ds(pl.multiple_of((cx * 6 + cy) * 64, 64), 64)
        v = [wide[slot * 64 : slot * 64 + 64, m * 128 : m * 128 + 128] for m in range(8)]
        for m in range(6):
            q_mat[rows, m * 128 : m * 128 + 128] = v[m + 1].astype(BF16)
        for m in range(7):
            q_mat[rows, 768 + m * 128 : 896 + m * 128] = jnp.where(low, v[m + 1], v[m]).astype(BF16)


def target_features(pos, soft, fs, ft):
    lane = iota((64, 128), 1)

    def put(f, v):
        for zp in range(6):
            fs[zp, pl.ds(f, 4, stride=16), :] = v[:, zp * 128 : zp * 128 + 128]

    for x in range(4):
        px, py, pz = (pos[d, x] - 0.5 for d in range(3))
        s = soft[x]
        fx = px + (x - 1.5)
        fy = py + (iota((4, 768), 0).astype(F32) - 1.5)
        ax, bx = pieces(fx, 2)
        ay, by = pieces(fy, 2)
        bx, by = bx.astype(BF16).astype(F32), by.astype(BF16).astype(F32)
        xx, yy = ax + bx, ay + by
        base = xx * xx + yy * yy + 0.5 * (s * s)
        for f, v in ((0, ax), (1, bx), (2, ax), (3, bx), (4, ay), (5, by), (6, ay), (7, by)):
            put(f, -2.0 * v)
        for f in (13, 14, 15):
            put(f, jnp.ones((4, 768), F32))
        for d in range(3):
            az, bz = pieces(pz - (d - 1.0), 2)
            bz = bz.astype(BF16).astype(F32)
            zz = az + bz
            n = base + zz * zz
            for f, v in zip((8, 9, 10, 11, 12), [-2.0 * az, -2.0 * bz] + pieces(n, 3)):
                put(f, v)
            for zp in range(6):
                made = fs[zp]
                if d != 1:
                    made = pltpu.roll(made, 64, 1)
                for e in range(2):
                    mine = lane < 64 if (e == 0) == (d == 1) else lane >= 64
                    half = jnp.where(mine, made, 0.0).astype(BF16)
                    for y in range(4):
                        ft[x * 4 + y, d, e, :, zp * 128 : zp * 128 + 128] = half[
                            y * 16 : y * 16 + 16
                        ]


Q_AT = (768, 0, 896)


def set_weights(b_mat, slot, ft, g):
    for k in range(3):
        for d in range(3):
            for h in range(2):
                for e in range(2):
                    cell = 4 * k + 2 + 2 * h + e + d - 1
                    r = (cell % 2) * 128 + (cell // 2) * 16
                    b_mat[slot, k * 3 + d, r : r + 16, h * 128 : h * 128 + 128] = ft[
                        g, d, e, :, (2 * k + h) * 128 : (2 * k + h) * 128 + 128
                    ]


def add_pairs(left, q_of, b_mat, slot, near8, g, own=None):
    rows = left.shape[0]
    for k in range(3):
        lanes = slice(256 * k, 256 * k + 256)
        for d in range(3):
            r2 = jnp.dot(left, b_mat[slot, k * 3 + d], preferred_element_type=F32)
            q = q_of(Q_AT[d] + 256 * k).astype(F32)
            if d == 1 and own is not None:
                q = q * own
            part = jnp.sum((lax.rsqrt(r2) * q).reshape(rows // 8, 8, 256), axis=0)
            if d == 0:
                swapped = part
            elif d == 1:
                plain = part
            else:
                swapped = swapped + part
        near8[g, 0, :, lanes] += plain
        near8[g, 1, :, lanes] += swapped


def slab_pairs(t, a_mat, q_mat, b_mat, ft, near8):
    x, dx = t // 3, lax.rem(t, 3)
    cx = x + dx
    itself = jnp.where(iota((64, 256), 0) == (iota((64, 256), 1) & 63), 0.0, 1.0).astype(F32)
    itself = jnp.where(dx == 1, itself, 1.0)
    one = jnp.ones((64, 256), F32)
    for y in range(4):
        low, high = max(1, y), min(4, y + 2)
        set_weights(b_mat, y, ft, x * 4 + y)
        rows = pl.ds(pl.multiple_of((cx * 6 + low) * 64, 64), (high - low + 1) * 64)
        own = jnp.concatenate([itself if cy == y + 1 else one for cy in range(low, high + 1)], axis=0)
        add_pairs(
            a_mat[rows, :], lambda at: q_mat[rows, at : at + 256], b_mat, y, near8, x * 4 + y, own
        )


def edge_pairs(x, a_mat, q_mat, b_mat, ft, near8):
    for slot, (y, cy) in enumerate(((0, 0), (3, 5))):
        set_weights(b_mat, slot, ft, x * 4 + y)
        rows = [pl.ds(pl.multiple_of(((x + i) * 6 + cy) * 64, 64), 64) for i in range(3)]
        add_pairs(
            jnp.concatenate([a_mat[r, :] for r in rows], axis=0),
            lambda at: jnp.concatenate([q_mat[r, at : at + 256] for r in rows], axis=0),
            b_mat, slot, near8, x * 4 + y,
        )


def gather_near(near8, near):
    for g in range(16):
        for zp in range(6):
            lanes = slice(zp * 128, zp * 128 + 128)
            both = near8[g, 0, :, lanes] + pltpu.roll(near8[g, 1, :, lanes], 64, 1)
            near[g : g + 1, lanes] = jnp.sum(both, axis=0, keepdims=True)


def far_kernel(
    gx, gy, gz,
    ml, ma, mb, t2, near, pos, cnt, top,
    pot_out, loc_out,
    lw, la, lb, lr, pa, ln,
):
    def shifted(v):
        return [v, pltpu.roll(v, 7, 0), pltpu.roll(v, 6, 0)]

    for xs in range(8):
        over_x = -1 if xs < 2 else (1 if xs >= 6 else 0)
        turned = []
        for yp in range(4):
            over_y = -1 if yp < 1 else (1 if yp >= 3 else 0)
            keep = jnp.where(inside(gx, over_x) & inside(gy, over_y), 1.0, 0.0).astype(F32)
            tile = ml[xs, yp].astype(F32) * keep
            turned.append((shifted(tile[0:8]), shifted(tile[8:16])))
        for w in range(6):
            for j in range(3):
                lw[xs, w, :, j * 128 : j * 128 + 128] = jnp.concatenate(
                    [turned[w // 2][w % 2][j], turned[w // 2 + 1][w % 2][j]], axis=0
                ).astype(BF16)
    zero8 = jnp.zeros((8, 128), F32)
    a_tiles = {}
    for xs in range(6):
        over_x = -1 if xs < 2 else (1 if xs >= 4 else 0)
        for yp in range(3):
            over_y = yp - 1
            keep = jnp.where(inside(gx, over_x) & inside(gy, over_y), 1.0, 0.0).astype(F32)
            tile = ma[xs, yp].astype(F32) * keep
            a_tiles[xs, yp] = (shifted(tile[0:8]), shifted(tile[8:16]))
    for dx in range(7):
        for w in range(6):
            for j in range(3):
                first = a_tiles[dx - 1, w // 2][w % 2][j] if dx >= 1 else zero8
                second = a_tiles[dx, w // 2][w % 2][j] if dx <= 5 else zero8
                la[dx, w, :, j * 128 : j * 128 + 128] = jnp.concatenate(
                    [first, second], axis=0
                ).astype(BF16)
    row16 = iota((16, 128), 0)
    odd_x, odd_y = lax.rem(gx, 2), lax.rem(gy, 2)
    for dx in range(7):
        ok_x = inside(gx, dx - 3)
        if dx == 0:
            ok_x = ok_x & (odd_x == 1)
        if dx == 6:
            ok_x = ok_x & (odd_x == 0)
        for w in range(6):
            dy = w + 1 - odd_y
            keep = jnp.where(ok_x & inside(gy, dy - 3), 1.0, 0.0).astype(F32)
            tile = mb[dx, dy].astype(F32) * keep
            for j in range(3):
                lb[dx, w, :, j * 128 : j * 128 + 128] = jnp.where(
                    (row16 >> 2) == j, tile, 0.0
                ).astype(BF16)

    total = [jnp.zeros((16, 256), F32) for _ in range(6)]
    for dx in range(7):
        xs_of = [x for x in range(4) if not (dx == 0 and x % 2 == 0) and not (dx == 6 and x % 2 == 1)]
        for w in range(6):
            g = dx * 7 + w + 1
            weights = jnp.concatenate(
                [t2[g * 384 : (g + 1) * 384, :], t2[(g - 1) * 384 : g * 384, :]], axis=1
            )
            left = [lw[x + dx - 1, w] for x in xs_of] + [la[dx, w], lb[dx, w]]
            made = jnp.dot(
                jnp.concatenate(left, axis=0), weights, preferred_element_type=F32
            )
            for i, slot in enumerate(xs_of + [4, 5]):
                total[slot] = total[slot] + made[i * 16 : i * 16 + 16]

    row, col = iota((64, 64), 0), iota((64, 64), 1)
    order = jnp.where(((row & 1) << 5) + (row >> 1) == col, 1.0, 0.0).astype(BF16)

    def ordered(v):
        return jnp.dot(v.astype(BF16), order, preferred_element_type=F32).astype(BF16)

    v_of = []
    for px in range(2):
        r = 49 * 384 + px * 128
        v_of.append(jnp.concatenate([t2[r : r + 64, :], t2[r + 64 : r + 128, :]], axis=1))
    sb = total[5]
    sb = sb[0:4] + sb[4:8] + sb[8:12]
    sb = jnp.where(odd_y == 1, sb[:, 128:256], sb[:, 0:128])
    parity = lax.rem(iota((4, 64), 0) + gz, 2)
    sb = jnp.where(parity == 1, sb[:, 64:128], sb[:, 0:64])
    topv = top[0]
    top4 = jnp.concatenate(
        [topv[:, 0:64], topv[:, 64:128], topv[:, 128:192], jnp.zeros((1, 64), F32)], axis=0
    )
    local_b = ordered(jnp.concatenate([top4 + 0.25 * sb, jnp.zeros((12, 64), F32)], axis=0))
    for xa in range(2):
        down = jnp.dot(local_b, v_of[xa], preferred_element_type=F32)[0:4]
        local_a = 0.5 * total[4][xa * 8 : xa * 8 + 4] + down
        for ya in range(2):
            for p in range(2):
                b = ya * 128 + p * 64
                pa[pl.ds(xa * 16 + ya * 8 + p, 4, stride=2), 0:64] = local_a[:, b : b + 64]
    for xa in range(2):
        parent = ordered(pa[xa * 16 : xa * 16 + 16, 0:64])
        for px in range(2):
            x = 2 * xa + px
            leaf = total[x] + jnp.dot(parent, v_of[px], preferred_element_type=F32)
            lr[x * 32 : x * 32 + 16, :] = leaf[:, 0:128]
            lr[x * 32 + 16 : x * 32 + 32, :] = leaf[:, 128:256]
    for x in range(4):
        for y in range(4):
            for zp in range(6):
                r = x * 32 + (y % 2) * 16 + (y // 2) * 8 + zp
                ln[x * 4 + y : x * 4 + y + 1, zp * 128 : zp * 128 + 128] = lr[r : r + 1, :]

    lane8 = iota((8, 128), 1)
    for i in range(2):
        for zp in range(6):
            lanes = slice(zp * 128, zp * 128 + 128)
            coef = ln[i * 8 : i * 8 + 8, lanes]
            cheb = []
            for d in range(3):
                u = 2.0 * jnp.concatenate(
                    [pos[d, 2 * i, :, lanes], pos[d, 2 * i + 1, :, lanes]], axis=0
                ) - 1.0
                t2nd = 2.0 * u * u - 1.0
                cheb.append([None, u, t2nd, 2.0 * u * t2nd - u])
            out = None
            for a in range(4):
                sum_b = None
                for b in range(4):
                    sum_c = None
                    for c in range(4):
                        index = (lane8 & 64) + (16 * a + 4 * b + c)
                        term = jnp.take_along_axis(coef, index, axis=1, mode="promise_in_bounds")
                        if c:
                            term = term * cheb[2][c]
                        sum_c = term if sum_c is None else sum_c + term
                    if b:
                        sum_c = sum_c * cheb[1][b]
                    sum_b = sum_c if sum_b is None else sum_b + sum_c
                if a:
                    sum_b = sum_b * cheb[0][a]
                out = sum_b if out is None else out + sum_b
            value = out * 0.125 + near[i * 8 : i * 8 + 8, lanes]
            limit, slot = count_lanes(
                jnp.concatenate([cnt[2 * i], cnt[2 * i + 1]], axis=0), zp
            )
            value = jnp.where(slot < limit, value, 0.0)
            for h in range(2):
                pot_out[2 * i + h, :, lanes] = value[h * 4 : h * 4 + 4]
                loc_out[2 * i + h, :, lanes] = coef[h * 4 : h * 4 + 4]


def whole_kernel(
    pos_in, chg_in, soft_in, cnt_in, top_in, bm_in, am_in, lm_in, m2l_in, l2l_in,
    pot_out, loc_out,
    t2, near, pos, cnt, top, lw, la, lb, lr, pa, ln,
    pf, ml, ma, mb, zs, zr, ps, mls, mas, ms, zf, mt, s2,
    chg, soft, bm, am, lm, l2l, a_mat, q_mat, b_mat, ft, fs, wt, near8,
    send, recv, local,
):
    gx, gy, gz = (lax.axis_index(a) for a in AXES)

    def at(ox, oy, oz):
        return (
            lax.rem(gx + (ox + 8), 8),
            lax.rem(gy + (oy + 8), 8),
            lax.rem(gz + (oz + 8), 8),
        )

    fetched = [(lm_in, lm), (am_in, am), (bm_in, bm), (pos_in, pos), (cnt_in, cnt)]
    fetched += [(chg_in, chg), (soft_in, soft), (l2l_in, l2l), (top_in, top), (m2l_in, mt)]
    fetched = [
        pltpu.make_async_copy(src, dst, local.at[i]) for i, (src, dst) in enumerate(fetched)
    ]
    for copy in fetched:
        copy.start()
    barrier = pltpu.get_barrier_semaphore()
    around = [at(0, 0, 1), at(0, 0, -1)]
    for o in (1, -1, 2, -2, 3, -3):
        around += [at(o, 0, 0), at(0, o, 0)]
    for who in around:
        pl.semaphore_signal(barrier, inc=1, device_id=who, device_id_type=MESH)

    number = [0]

    def remote(src, dst, who):
        i = number[0]
        number[0] += 1
        copy = pltpu.make_async_remote_copy(
            src_ref=src, dst_ref=dst, send_sem=send.at[i], recv_sem=recv.at[i],
            device_id=who, device_id_type=MESH,
        )
        copy.start()
        return copy

    for copy in fetched[:3]:
        copy.wait()
    for x in range(4):
        block = lm[x].astype(F32)
        for zp in range(6):
            ms[zp * 16 + x * 4 : zp * 16 + x * 4 + 4, :] = block[:, zp * 128 : zp * 128 + 128]
    for x in range(2):
        block = am[x].astype(F32)
        for zp in range(3):
            ms[96 + zp * 4 + x * 2 : 98 + zp * 4 + x * 2, :] = block[:, zp * 128 : zp * 128 + 128]
    bcells = bm[0].astype(F32)
    ms[108:109, :] = bcells[:, 0:128]
    ms[109:110, :] = jnp.concatenate([bcells[:, 64:128], bcells[:, 128:192]], axis=1)
    ms[110:112, :] = jnp.zeros((2, 128), F32)
    row, col = iota((128, 128), 0), iota((128, 128), 1)
    moved = (row & 64) + ((row & 1) << 5) + ((row & 63) >> 1)
    order = jnp.where(moved == col, 1.0, 0.0).astype(BF16)
    ms[...] = jnp.dot(ms[...].astype(BF16), order, preferred_element_type=F32)

    for copy in fetched[3:7]:
        copy.wait()
    ps[...] = jnp.zeros_like(ps)
    mas[...] = jnp.zeros_like(mas)
    zf[...] = jnp.zeros_like(zf)
    for x in range(4):
        fields = [pos[0, x] - 0.5, pos[1, x] - 0.5, pos[2, x] - 0.5, chg[x], soft[x]]
        counts = cnt[x]
        for zp in range(6):
            limit, slot = count_lanes(counts, zp)
            for f in range(5):
                piece = fields[f][:, zp * 128 : zp * 128 + 128]
                if f == 3:
                    piece = jnp.where(slot < limit, piece, 0.0)
                ps[pl.ds(x * 192 + f * 8 + 1 + zp, 4, stride=48), :] = piece
                if zp == 0:
                    zf[f * 16 + x * 4 : f * 16 + x * 4 + 4, :] = piece
                if zp == 5:
                    zf[112 + f * 16 + x * 4 : 112 + f * 16 + x * 4 + 4, :] = piece
    for side, (lp, ap) in enumerate(((0, 0), (5, 2))):
        base = side * 112
        zf[base + 80 : base + 96, :] = ms[lp * 16 : lp * 16 + 16, :]
        zf[base + 96 : base + 100, :] = ms[96 + ap * 4 : 100 + ap * 4, :]
        zf[base + 100 : base + 102, :] = ms[108:110, :]
        zs[side] = zf[base : base + 112, :].astype(BF16)
    pl.semaphore_wait(barrier, 14)

    z_copies = [
        remote(zs.at[0], zr.at[1], at(0, 0, -1)),
        remote(zs.at[1], zr.at[0], at(0, 0, 1)),
    ]
    for zp in range(6):
        for x in range(4):
            mls[pl.ds(x * 32 + zp + 1, 4, stride=8), :] = ms[
                zp * 16 + x * 4 : zp * 16 + x * 4 + 4, :
            ]
    for zp in range(3):
        for x in range(2):
            mas[pl.ds(x * 16 + zp + 1, 2, stride=8), :] = ms[
                96 + zp * 4 + x * 2 : 98 + zp * 4 + x * 2, :
            ]

    near8[...] = jnp.zeros_like(near8)
    b_mat[...] = jnp.zeros_like(b_mat)
    wt[...] = jnp.zeros_like(wt)
    target_features(pos, soft, fs, ft)

    for copy in fetched[7:]:
        copy.wait()

    def unpack(i, carry):
        block = mt[pl.ds(pl.multiple_of(i * 16, 16), 16), :].astype(F32)
        unpack_rows(block, i * 16, s2, 16)
        return carry

    lax.fori_loop(0, 21, unpack, 0)
    unpack_rows(mt[336:343, :].astype(F32), 336, s2, 7)
    unpack_rows(l2l[...].astype(F32), 343, s2, 8)

    for copy in z_copies:
        copy.wait()
    keep_low = jnp.where(gz > 0, 1.0, 0.0).astype(F32)
    keep_high = jnp.where(gz < 7, 1.0, 0.0).astype(F32)
    b_rows = []
    for side, (keep, zp_l, zp_a) in enumerate(((keep_low, 0, 0), (keep_high, 7, 4))):
        got = zr[side].astype(F32) * keep
        for x in range(4):
            for f in range(5):
                ps[pl.ds(x * 192 + f * 8 + zp_l, 4, stride=48), :] = got[
                    f * 16 + x * 4 : f * 16 + x * 4 + 4, :
                ]
            mls[pl.ds(x * 32 + zp_l, 4, stride=8), :] = got[80 + x * 4 : 84 + x * 4, :]
        for x in range(2):
            mas[pl.ds(x * 16 + zp_a, 2, stride=8), :] = got[96 + x * 2 : 98 + x * 2, :]
        b_rows.append((got[100:101, :], got[101:102, :]))
    (left_a, left_b), (ra, rb) = b_rows
    oa, ob = ms[108:109, :], ms[109:110, :]
    low1 = iota((1, 128), 1) < 64
    middle = jnp.where(low1, pltpu.roll(left_b, 64, 1), pltpu.roll(oa, 64, 1))
    middle_r = jnp.where(low1, pltpu.roll(ob, 64, 1), pltpu.roll(ra, 64, 1))
    pairs = [left_a, left_b, middle, oa, ob, middle_r, ra, rb]
    even_z = lax.rem(gz, 2) == 0
    zf[0:16, :] = jnp.zeros((16, 128), F32)
    for l in range(3):
        at_even = l + 1 - l % 2
        at_odd = l + 1 - (l + 1) % 2
        for j in range(3):
            zf[4 * j + l : 4 * j + l + 1, :] = jnp.where(
                even_z, pairs[at_even + 2 * j], pairs[at_odd + 2 * j]
            )
    mb[3, 3] = zf[0:16, :].astype(BF16)
    x_b = []
    for o in (1, -1, 2, -2, 3, -3):
        x_b.append(remote(mb.at[3, 3], mb.at[3 - o, 3], at(o, 0, 0)))
    for x in range(4):
        for y in range(4):
            for t in range(3):
                r = (x * 4 + y) * 48 + t * 16
                pf[1 + x, 1 + y, t] = ps[r : r + 16, :].astype(BF16)
        for yp in range(2):
            r = x * 32 + yp * 16
            ml[2 + x, 1 + yp] = mls[r : r + 16, :].astype(BF16)
    for x in range(2):
        ma[2 + x, 1] = mas[x * 16 : x * 16 + 16, :].astype(BF16)

    own_x, own_xl, own_xa = pl.ds(1, 4), pl.ds(2, 4), pl.ds(2, 2)
    up, down = at(0, 1, 0), at(0, -1, 0)
    y_copies = [
        remote(pf.at[own_x, pl.ds(4, 1)], pf.at[own_x, pl.ds(0, 1)], up),
        remote(pf.at[own_x, pl.ds(1, 1)], pf.at[own_x, pl.ds(5, 1)], down),
        remote(ml.at[own_xl, pl.ds(2, 1)], ml.at[own_xl, pl.ds(0, 1)], up),
        remote(ml.at[own_xl, pl.ds(1, 1)], ml.at[own_xl, pl.ds(3, 1)], down),
        remote(ma.at[own_xa, pl.ds(1, 1)], ma.at[own_xa, pl.ds(0, 1)], up),
        remote(ma.at[own_xa, pl.ds(1, 1)], ma.at[own_xa, pl.ds(2, 1)], down),
    ]

    low_lanes = iota((32, 128), 1) < 64

    def pair_up(g, carry):
        near = (jnp.abs(g // 7 - 3) <= 1) & (jnp.abs(lax.rem(g, 7) - 3) <= 1)
        kept = jnp.where(near, 0.0, 1.0).astype(F32)
        tables = []
        for i in range(7):
            one = s2[pl.ds(pl.multiple_of((g * 7 + i) * 32, 32), 32), :]
            if 2 <= i <= 4:
                one = one * kept
            tables.append((one, pltpu.roll(one, 64, 1)))
        for w in range(6):
            (first, turned_first), (second, turned_second) = tables[w + 1], tables[w]
            to = g * 384 + w * 64
            t2[pl.ds(pl.multiple_of(to, 32), 32), :] = jnp.where(
                low_lanes, first, turned_second
            ).astype(BF16)
            t2[pl.ds(pl.multiple_of(to + 32, 32), 32), :] = jnp.where(
                low_lanes, turned_first, second
            ).astype(BF16)
        return carry

    def own_columns(i, carry):
        source_columns([(i, cy) for cy in range(1, 5)], gx, gy, pf, wt, a_mat, q_mat)
        return carry

    lax.fori_loop(1, 5, own_columns, 0)
    for copy in x_b:
        copy.wait()
    y_b = []
    for o in (1, -1, 2, -2, 3, -3):
        y_b.append(remote(mb.at[:, pl.ds(3, 1)], mb.at[:, pl.ds(3 - o, 1)], at(0, o, 0)))
    for copy in y_copies:
        copy.wait()

    up, down = at(1, 0, 0), at(-1, 0, 0)
    x_copies = [
        remote(pf.at[pl.ds(4, 1)], pf.at[pl.ds(0, 1)], up),
        remote(pf.at[pl.ds(1, 1)], pf.at[pl.ds(5, 1)], down),
        remote(ml.at[pl.ds(4, 2)], ml.at[pl.ds(0, 2)], up),
        remote(ml.at[pl.ds(2, 2)], ml.at[pl.ds(6, 2)], down),
        remote(ma.at[pl.ds(2, 2)], ma.at[pl.ds(0, 2)], up),
        remote(ma.at[pl.ds(2, 2)], ma.at[pl.ds(4, 2)], down),
    ]
    def own_pairs(t, carry):
        slab_pairs(t, a_mat, q_mat, b_mat, ft, near8)
        for u in range(5):
            pair_up(jnp.minimum((t - 1) * 5 + u, 48), 0)
        return carry

    lax.fori_loop(1, 11, own_pairs, 0)
    for child in range(4):
        r = (343 + 2 * child) * 32
        even, odd = pair_rows(s2[r : r + 32, :], s2[r + 32 : r + 64, :], low_lanes)
        to = 49 * 384 + child * 64
        t2[to : to + 32, :] = even
        t2[to + 32 : to + 64, :] = odd
    for copy in x_copies + y_b:
        copy.wait()

    def columns_y(i, carry):
        source_columns([(i, 0), (i, 5)], gx, gy, pf, wt, a_mat, q_mat)
        return carry

    def columns_x(i, carry):
        source_columns([(i * 5, cy) for cy in range(6)], gx, gy, pf, wt, a_mat, q_mat)
        return carry

    def slab_edges(i, carry):
        slab_pairs(i * 11, a_mat, q_mat, b_mat, ft, near8)
        return carry

    def row_edges(x, carry):
        edge_pairs(x, a_mat, q_mat, b_mat, ft, near8)
        return carry

    lax.fori_loop(1, 5, columns_y, 0)
    lax.fori_loop(0, 2, columns_x, 0)
    lax.fori_loop(0, 2, slab_edges, 0)
    lax.fori_loop(0, 4, row_edges, 0)
    gather_near(near8, near)
    far_kernel(
        gx, gy, gz, ml, ma, mb, t2, near, pos, cnt, top, pot_out, loc_out, lw, la, lb, lr, pa, ln
    )


NEAR_SCRATCH = [
    ((2304, 256), BF16),
    ((2304, 1664), BF16),
    ((4, 9, 256, 256), BF16),
    ((16, 3, 2, 16, 768), BF16),
    ((6, 64, 128), F32),
    ((6, 144, 128), F32),
    ((16, 2, 8, 768), F32),
]


FAR_SCRATCH = [
    ((8, 6, 16, 384), BF16),
    ((7, 6, 16, 384), BF16),
    ((7, 6, 16, 384), BF16),
    ((128, 128), F32),
    ((32, 128), F32),
    ((16, 768), F32),
]


def run(*args):
    halos = [(6, 6, 3, 16, 128), (8, 4, 16, 128), (6, 3, 16, 128), (7, 7, 16, 128)]
    scratch = [((T2_ROWS, 128), BF16), ((16, 768), F32), ((3, 4, 4, 768), F32)]
    scratch += [((4, 4, 12), jnp.int32), ((1, 1, 192), F32)] + FAR_SCRATCH
    scratch += [(s, BF16) for s in halos]
    scratch += [((2, 112, 128), BF16), ((2, 112, 128), BF16), ((768, 128), F32), ((128, 128), F32)]
    scratch += [((32, 128), F32), ((112, 128), F32), ((224, 128), F32), ((343, 4096), BF16)]
    scratch += [((352 * 32, 128), F32), ((4, 4, 768), F32), ((4, 4, 768), F32)]
    scratch += [((1, 1, 192), BF16), ((2, 2, 384), BF16), ((4, 4, 768), BF16), ((8, 4096), BF16)]
    return pl.pallas_call(
        whole_kernel,
        name="downward",
        out_shape=[jax.ShapeDtypeStruct((4, 4, 768), F32)] * 2,
        in_specs=[pl.BlockSpec(memory_space=pltpu.HBM)] * 10,
        out_specs=[pl.BlockSpec(memory_space=pltpu.VMEM)] * 2,
        scratch_shapes=[pltpu.VMEM(s, t) for s, t in scratch + NEAR_SCRATCH]
        + [
            pltpu.SemaphoreType.DMA((26,)),
            pltpu.SemaphoreType.DMA((26,)),
            pltpu.SemaphoreType.DMA((10,)),
        ],
        compiler_params=pltpu.CompilerParams(
            collective_id=0, has_side_effects=True, vmem_limit_bytes=VMEM_BYTES
        ),
        cost_estimate=pl.CostEstimate(
            flops=10**10, bytes_accessed=10**7, transcendentals=2 * 10**7
        ),
    )(*args)


def per_device(pos, chg, soft, cnt, top, bm, am, lm, m2l, l2l):
    return tuple(run(pos, chg, soft, cnt, top, bm, am, lm, m2l, l2l))


def solution(mesh):
    split = P("gx", "gy", "gz")
    in_specs = (P(None, "gx", "gy", "gz"),) + (split,) * 7 + (P(), P())
    return jax.shard_map(
        per_device, mesh=mesh, in_specs=in_specs, out_specs=(split, split), check_vma=False
    )
```

time: 67.8 us -> 54 us (0.80)
  local copies, waits for them, and re-layouts: 11 us -> 2.84 us
  Pallas kernels: 55.5 us -> 50.2 us
    unnamed x26 -> x2, local copies, waits for them, and re-layouts: 11 us -> 2.84 us
    pallas_call x2 -> x1, Pallas kernels: 55.5 us -> 50.2 us  [run(): pl.pallas_call(whole_kernel, name='downward', out_shape=[jax.ShapeDtypeSt...]
where the time goes in v1:
time: 54 us; the launch traced here: 53.7 us
  Pallas kernels  50.2 us (93%)
  local copies, waits for them, and re-layouts  2.84 us (5%)
  between operations  0.64 us (1%)
    pallas_call x1, Pallas kernels, run(): pl.pallas_call(whole_kernel, name='downward', out_shape=[jax.ShapeDtypeSt...  50.2 us
    unnamed x2, local copies, waits for them, and re-layouts  2.84 us

profile of v1, /device:TPU:1, one launch (start us, length us, event | category | flops | bytes accessed | tf_op | source)
XLA Modules:
  0.0 53.7 jit_solution(11650576984112637209)
XLA Ops:
  0.6 50.2 %downward.1 = (f32[4,4,768]{2,1,0:T(4,128)}, f32[4,4,768]{2,1,0:T(4,128)}) custom-call(f32[3,4,4,768]{3,2,1,0:T(4,128)} %pos_in.1, f32[4,4,768]{2,1,0:T(4,128)} %chg_in.1, f32[4,4,768]{2,1,0:T(4,128)} %soft_in.1, s32[4,4,12]{2,1,0:T(4,128)} %cnt_in.1, f32[1,1,192]{2,1,0:T(1,128)} %top_in.1, bf16[1,1,192]{2,1,0:T(2,128)(2,1)} %bm_in.1, ...), custom_call_target="tpu_custom_call" | custom-call | flops 10000000000 | bytes 10000000 | tf_op jit(solution)/shard_map/downward/pallas_call | solution.py:654
  50.8 1.4 %copy.14 = f32[4,4,768]{2,1,0:T(4,128)} copy(f32[4,4,768]{2,1,0:T(4,128)} %get-tuple-element.4) | data formatting | bytes 98304
  52.2 1.4 %copy.15 = f32[4,4,768]{2,1,0:T(4,128)} copy(f32[4,4,768]{2,1,0:T(4,128)} %get-tuple-element.5) | data formatting | bytes 98304

commit v2 on v1

--- a/solution.py
+++ b/solution.py
@@ -52,13 +52,14 @@
     return (coord + offset >= 0) & (coord + offset <= 7)
 
 
-def source_columns(where, gx, gy, pf, wt, a_mat, q_mat):
+def source_columns(where, gx, gy, pf, wt, base=0):
     ones = jnp.ones((8, 128), F32)
     same = jnp.where(iota((128, 128), 0) == iota((128, 128), 1), 1.0, 0.0).astype(BF16)
     er, ec = iota((16, 1024), 0), iota((16, 1024), 1)
     spread = jnp.where(((er & 7) * 2 + (er >> 3)) == (ec >> 6), 1.0, 0.0).astype(BF16)
     charges = []
-    for slot, (cx, cy) in enumerate(where):
+    for slot, (cx, cy, _, _, _) in enumerate(where):
+        slot = slot + base
         xy = pf[cx, cy, 0].astype(F32)
         zq = pf[cx, cy, 1].astype(F32)
         s = pf[cx, cy, 2].astype(F32)[0:8]
@@ -73,11 +74,11 @@
         for f in range(16):
             wt[slot, pl.ds(f, 8, stride=16), :] = feats[f]
         wt[slot, 128:136, :] = q
-    for slot, (cx, cy) in enumerate(where):
+    for slot, (_, _, a_mat, q_mat, at) in enumerate(where):
         turned = lax.dot_general(
-            same, wt[slot].astype(BF16), (((1,), (1,)), ((), ())), preferred_element_type=F32
+            same, wt[slot + base].astype(BF16), (((1,), (1,)), ((), ())), preferred_element_type=F32
         )
-        rows = pl.ds(pl.multiple_of((cx * 6 + cy) * 64, 64), 64)
+        rows = pl.ds(pl.multiple_of(at * 64, 64), 64)
         a_mat[rows, 0:128] = turned[0:64, 0:128].astype(BF16)
         a_mat[rows, 128:256] = turned[64:128, 0:128].astype(BF16)
         charges.append(
@@ -87,8 +88,8 @@
         jnp.concatenate(charges, axis=0).astype(BF16), spread, preferred_element_type=F32
     )
     low = iota((64, 128), 1) < 64
-    for slot, (cx, cy) in enumerate(where):
-        rows = pl.ds(pl.multiple_of((cx * 6 + cy) * 64, 64), 64)
+    for slot, (_, _, a_mat, q_mat, at) in enumerate(where):
+        rows = pl.ds(pl.multiple_of(at * 64, 64), 64)
         v = [wide[slot * 64 : slot * 64 + 64, m * 128 : m * 128 + 128] for m in range(8)]
         for m in range(6):
             q_mat[rows, m * 128 : m * 128 + 128] = v[m + 1].astype(BF16)
@@ -172,30 +173,35 @@
         near8[g, 1, :, lanes] += swapped
 
 
-def slab_pairs(t, a_mat, q_mat, b_mat, ft, near8):
-    x, dx = t // 3, lax.rem(t, 3)
-    cx = x + dx
-    itself = jnp.where(iota((64, 256), 0) == (iota((64, 256), 1) & 63), 0.0, 1.0).astype(F32)
-    itself = jnp.where(dx == 1, itself, 1.0)
+def slab_pairs(x, itself, a_mat, q_mat, at, b_mat, ft, near8):
     one = jnp.ones((64, 256), F32)
     for y in range(4):
-        low, high = max(1, y), min(4, y + 2)
+        low, high = max(0, y - 1), min(3, y + 1)
         set_weights(b_mat, y, ft, x * 4 + y)
-        rows = pl.ds(pl.multiple_of((cx * 6 + low) * 64, 64), (high - low + 1) * 64)
-        own = jnp.concatenate([itself if cy == y + 1 else one for cy in range(low, high + 1)], axis=0)
+        rows = pl.ds(pl.multiple_of((at + low) * 64, 64), (high - low + 1) * 64)
+        own = None
+        if itself is not None:
+            own = jnp.concatenate(
+                [itself if cy == y else one for cy in range(low, high + 1)], axis=0
+            )
         add_pairs(
             a_mat[rows, :], lambda at: q_mat[rows, at : at + 256], b_mat, y, near8, x * 4 + y, own
         )
 
 
-def edge_pairs(x, a_mat, q_mat, b_mat, ft, near8):
-    for slot, (y, cy) in enumerate(((0, 0), (3, 5))):
-        set_weights(b_mat, slot, ft, x * 4 + y)
-        rows = [pl.ds(pl.multiple_of(((x + i) * 6 + cy) * 64, 64), 64) for i in range(3)]
+def own_slab(t, a_own, q_own, b_mat, ft, near8):
+    x, dx = t // 3, lax.rem(t, 3)
+    itself = jnp.where(iota((64, 256), 0) == (iota((64, 256), 1) & 63), 0.0, 1.0).astype(F32)
+    itself = jnp.where(dx == 1, itself, 1.0)
+    slab_pairs(x, itself, a_own, q_own, (x + dx - 1) * 4, b_mat, ft, near8)
+
+
+def edge_pairs(x, a_edge, q_edge, b_mat, ft, near8):
+    for side, y in enumerate((0, 3)):
+        set_weights(b_mat, 4 + side, ft, x * 4 + y)
+        rows = pl.ds(pl.multiple_of((side * 6 + x) * 64, 64), 192)
         add_pairs(
-            jnp.concatenate([a_mat[r, :] for r in rows], axis=0),
-            lambda at: jnp.concatenate([q_mat[r, at : at + 256] for r in rows], axis=0),
-            b_mat, slot, near8, x * 4 + y,
+            a_edge[rows, :], lambda at: q_edge[rows, at : at + 256], b_mat, 4 + side, near8, x * 4 + y
         )
 
 
@@ -211,7 +217,7 @@
     gx, gy, gz,
     ml, ma, mb, t2, near, pos, cnt, top,
     pot_out, loc_out,
-    lw, la, lb, lr, pa, ln,
+    lw, la, lb, lr, pa, ln, to_lanes,
 ):
     def shifted(v):
         return [v, pltpu.roll(v, 7, 0), pltpu.roll(v, 6, 0)]
@@ -318,51 +324,64 @@
                 r = x * 32 + (y % 2) * 16 + (y // 2) * 8 + zp
                 ln[x * 4 + y : x * 4 + y + 1, zp * 128 : zp * 128 + 128] = lr[r : r + 1, :]
 
-    lane8 = iota((8, 128), 1)
-    for i in range(2):
-        for zp in range(6):
-            lanes = slice(zp * 128, zp * 128 + 128)
-            coef = ln[i * 8 : i * 8 + 8, lanes]
-            cheb = []
-            for d in range(3):
-                u = 2.0 * jnp.concatenate(
-                    [pos[d, 2 * i, :, lanes], pos[d, 2 * i + 1, :, lanes]], axis=0
-                ) - 1.0
-                t2nd = 2.0 * u * u - 1.0
-                cheb.append([None, u, t2nd, 2.0 * u * t2nd - u])
-            out = None
-            for a in range(4):
-                sum_b = None
-                for b in range(4):
-                    sum_c = None
-                    for c in range(4):
-                        index = (lane8 & 64) + (16 * a + 4 * b + c)
-                        term = jnp.take_along_axis(coef, index, axis=1, mode="promise_in_bounds")
-                        if c:
-                            term = term * cheb[2][c]
-                        sum_c = term if sum_c is None else sum_c + term
-                    if b:
-                        sum_c = sum_c * cheb[1][b]
-                    sum_b = sum_c if sum_b is None else sum_b + sum_c
-                if a:
-                    sum_b = sum_b * cheb[0][a]
-                out = sum_b if out is None else out + sum_b
-            value = out * 0.125 + near[i * 8 : i * 8 + 8, lanes]
-            limit, slot = count_lanes(
-                jnp.concatenate([cnt[2 * i], cnt[2 * i + 1]], axis=0), zp
-            )
-            value = jnp.where(slot < limit, value, 0.0)
-            for h in range(2):
-                pot_out[2 * i + h, :, lanes] = value[h * 4 : h * 4 + 4]
-                loc_out[2 * i + h, :, lanes] = coef[h * 4 : h * 4 + 4]
+    coef = jnp.concatenate([ln[:, zp * 128 : zp * 128 + 128] for zp in range(6)], axis=0)
+    high, low = pieces(coef, 2)
+    coef = jnp.concatenate([high.astype(BF16), low.astype(BF16)], axis=1)
+    cheb = []
+    for d in range(3):
+        u = 2.0 * jnp.concatenate(
+            [pos[d, x, :, zp * 128 : zp * 128 + 128] for zp in range(6) for x in range(4)], axis=0
+        ) - 1.0
+        second = 2.0 * u * u - 1.0
+        cheb.append([None, u, second, 2.0 * u * second - u])
+    out = None
+    for a in range(4):
+        spread = jnp.dot(
+            coef, to_lanes[:, a * 2048 : a * 2048 + 2048], preferred_element_type=F32
+        )
+        sum_b = None
+        for b in range(4):
+            sum_c = None
+            for c in range(4):
+                term = spread[:, (4 * b + c) * 128 : (4 * b + c) * 128 + 128]
+                if c:
+                    term = term * cheb[2][c]
+                sum_c = term if sum_c is None else sum_c + term
+            if b:
+                sum_c = sum_c * cheb[1][b]
+            sum_b = sum_c if sum_b is None else sum_b + sum_c
+        if a:
+            sum_b = sum_b * cheb[0][a]
+        out = sum_b if out is None else out + sum_b
+    for zp in range(6):
+        lanes = slice(zp * 128, zp * 128 + 128)
+        value = out[zp * 16 : zp * 16 + 16] * 0.125 + near[:, lanes]
+        for x in range(4):
+            limit, slot = count_lanes(cnt[x], zp)
+            pot_out[x, :, lanes] = jnp.where(slot < limit, value[x * 4 : x * 4 + 4], 0.0)
+            loc_out[x, :, lanes] = ln[x * 4 : x * 4 + 4, lanes]
+
+
+def lane_spread(to_lanes):
+    row, col = iota((128, 128), 0), iota((128, 128), 1)
+
+    def one(c, carry):
+        block = jnp.where(row == (col & 64) + c, 1.0, 0.0).astype(BF16)
+        lanes = pl.ds(pl.multiple_of(c * 128, 128), 128)
+        to_lanes[0:128, lanes] = block
+        to_lanes[128:256, lanes] = block
+        return carry
+
+    lax.fori_loop(0, 64, one, 0)
 
 
 def whole_kernel(
     pos_in, chg_in, soft_in, cnt_in, top_in, bm_in, am_in, lm_in, m2l_in, l2l_in,
     pot_out, loc_out,
-    t2, near, pos, cnt, top, lw, la, lb, lr, pa, ln,
+    t2, near, pos, cnt, top, lw, la, lb, lr, pa, ln, to_lanes,
     pf, ml, ma, mb, zs, zr, ps, mls, mas, ms, zf, mt, s2,
-    chg, soft, bm, am, lm, l2l, a_mat, q_mat, b_mat, ft, fs, wt, near8,
+    chg, soft, bm, am, lm, l2l,
+    a_own, q_own, a_side, q_side, a_edge, q_edge, b_mat, ft, fs, wt, near8,
     send, recv, local,
 ):
     gx, gy, gz = (lax.axis_index(a) for a in AXES)
@@ -421,25 +440,23 @@
 
     for copy in fetched[3:7]:
         copy.wait()
-    ps[...] = jnp.zeros_like(ps)
-    mas[...] = jnp.zeros_like(mas)
+    own = []
+    for x in range(4):
+        own.append([pos[0, x] - 0.5, pos[1, x] - 0.5, pos[2, x] - 0.5, chg[x], soft[x]])
+
+    def own_piece(x, f, zp):
+        piece = own[x][f][:, zp * 128 : zp * 128 + 128]
+        if f == 3:
+            limit, slot = count_lanes(cnt[x], zp)
+            piece = jnp.where(slot < limit, piece, 0.0)
+        return piece
+
     zf[...] = jnp.zeros_like(zf)
-    for x in range(4):
-        fields = [pos[0, x] - 0.5, pos[1, x] - 0.5, pos[2, x] - 0.5, chg[x], soft[x]]
-        counts = cnt[x]
-        for zp in range(6):
-            limit, slot = count_lanes(counts, zp)
-            for f in range(5):
-                piece = fields[f][:, zp * 128 : zp * 128 + 128]
-                if f == 3:
-                    piece = jnp.where(slot < limit, piece, 0.0)
-                ps[pl.ds(x * 192 + f * 8 + 1 + zp, 4, stride=48), :] = piece
-                if zp == 0:
-                    zf[f * 16 + x * 4 : f * 16 + x * 4 + 4, :] = piece
-                if zp == 5:
-                    zf[112 + f * 16 + x * 4 : 112 + f * 16 + x * 4 + 4, :] = piece
     for side, (lp, ap) in enumerate(((0, 0), (5, 2))):
         base = side * 112
+        for x in range(4):
+            for f in range(5):
+                zf[base + f * 16 + x * 4 : base + f * 16 + x * 4 + 4, :] = own_piece(x, f, lp)
         zf[base + 80 : base + 96, :] = ms[lp * 16 : lp * 16 + 16, :]
         zf[base + 96 : base + 100, :] = ms[96 + ap * 4 : 100 + ap * 4, :]
         zf[base + 100 : base + 102, :] = ms[108:110, :]
@@ -450,6 +467,12 @@
         remote(zs.at[0], zr.at[1], at(0, 0, -1)),
         remote(zs.at[1], zr.at[0], at(0, 0, 1)),
     ]
+    ps[...] = jnp.zeros_like(ps)
+    mas[...] = jnp.zeros_like(mas)
+    for x in range(4):
+        for zp in range(6):
+            for f in range(5):
+                ps[pl.ds(x * 192 + f * 8 + 1 + zp, 4, stride=48), :] = own_piece(x, f, zp)
     for zp in range(6):
         for x in range(4):
             mls[pl.ds(x * 32 + zp + 1, 4, stride=8), :] = ms[
@@ -465,6 +488,7 @@
     b_mat[...] = jnp.zeros_like(b_mat)
     wt[...] = jnp.zeros_like(wt)
     target_features(pos, soft, fs, ft)
+    lane_spread(to_lanes)
 
     for copy in fetched[7:]:
         copy.wait()
@@ -558,10 +582,21 @@
         return carry
 
     def own_columns(i, carry):
-        source_columns([(i, cy) for cy in range(1, 5)], gx, gy, pf, wt, a_mat, q_mat)
+        where = [(i, cy, a_own, q_own, (i - 1) * 4 + cy - 1) for cy in range(1, 5)]
+        source_columns(where, gx, gy, pf, wt)
         return carry
 
+    def pair_some(i):
+        for u in range(6):
+            pair_up(jnp.minimum(i * 6 + u, 48), 0)
+
+    def own_pairs(t, carry):
+        own_slab(t, a_own, q_own, b_mat, ft, near8)
+        pair_some(t - 1)
+        return carry
+
     lax.fori_loop(1, 5, own_columns, 0)
+    lax.fori_loop(1, 5, own_pairs, 0)
     for copy in x_b:
         copy.wait()
     y_b = []
@@ -579,13 +614,16 @@
         remote(ma.at[pl.ds(2, 2)], ma.at[pl.ds(0, 2)], up),
         remote(ma.at[pl.ds(2, 2)], ma.at[pl.ds(4, 2)], down),
     ]
-    def own_pairs(t, carry):
-        slab_pairs(t, a_mat, q_mat, b_mat, ft, near8)
-        for u in range(5):
-            pair_up(jnp.minimum((t - 1) * 5 + u, 48), 0)
+    def own_pairs_y(t, carry):
+        cx = t - 4
+        where = [(cx, 0, a_edge, q_edge, cx), (cx, 5, a_edge, q_edge, cx + 6)]
+        source_columns(where, gx, gy, pf, wt)
+        own_slab(t, a_own, q_own, b_mat, ft, near8)
+        pair_some(t - 1)
         return carry
 
-    lax.fori_loop(1, 11, own_pairs, 0)
+    lax.fori_loop(5, 9, own_pairs_y, 0)
+    pair_up(48, 0)
     for child in range(4):
         r = (343 + 2 * child) * 32
         even, odd = pair_rows(s2[r : r + 32, :], s2[r + 32 : r + 64, :], low_lanes)
@@ -595,36 +633,37 @@
     for copy in x_copies + y_b:
         copy.wait()
 
-    def columns_y(i, carry):
-        source_columns([(i, 0), (i, 5)], gx, gy, pf, wt, a_mat, q_mat)
+    def own_pairs_x(i, carry):
+        cx = i * 5
+        where = [(cx, 0, a_edge, q_edge, cx), (cx, 5, a_edge, q_edge, cx + 6)]
+        where += [(cx, cy, a_side, q_side, i * 4 + cy - 1) for cy in range(1, 5)]
+        source_columns(where, gx, gy, pf, wt)
+        own_slab(i + 9, a_own, q_own, b_mat, ft, near8)
+        edge_pairs(i + 1, a_edge, q_edge, b_mat, ft, near8)
         return carry
 
-    def columns_x(i, carry):
-        source_columns([(i * 5, cy) for cy in range(6)], gx, gy, pf, wt, a_mat, q_mat)
+    def last_pairs(i, carry):
+        slab_pairs(i * 3, None, a_side, q_side, i * 4, b_mat, ft, near8)
+        edge_pairs(i * 3, a_edge, q_edge, b_mat, ft, near8)
         return carry
 
-    def slab_edges(i, carry):
-        slab_pairs(i * 11, a_mat, q_mat, b_mat, ft, near8)
-        return carry
-
-    def row_edges(x, carry):
-        edge_pairs(x, a_mat, q_mat, b_mat, ft, near8)
-        return carry
-
-    lax.fori_loop(1, 5, columns_y, 0)
-    lax.fori_loop(0, 2, columns_x, 0)
-    lax.fori_loop(0, 2, slab_edges, 0)
-    lax.fori_loop(0, 4, row_edges, 0)
+    lax.fori_loop(0, 2, own_pairs_x, 0)
+    lax.fori_loop(0, 2, last_pairs, 0)
     gather_near(near8, near)
     far_kernel(
-        gx, gy, gz, ml, ma, mb, t2, near, pos, cnt, top, pot_out, loc_out, lw, la, lb, lr, pa, ln
+        gx, gy, gz, ml, ma, mb, t2, near, pos, cnt, top, pot_out, loc_out,
+        lw, la, lb, lr, pa, ln, to_lanes,
     )
 
 
 NEAR_SCRATCH = [
-    ((2304, 256), BF16),
-    ((2304, 1664), BF16),
-    ((4, 9, 256, 256), BF16),
+    ((1024, 256), BF16),
+    ((1024, 1664), BF16),
+    ((512, 256), BF16),
+    ((512, 1664), BF16),
+    ((768, 256), BF16),
+    ((768, 1664), BF16),
+    ((6, 9, 256, 256), BF16),
     ((16, 3, 2, 16, 768), BF16),
     ((6, 64, 128), F32),
     ((6, 144, 128), F32),
@@ -639,6 +678,7 @@
     ((128, 128), F32),
     ((32, 128), F32),
     ((16, 768), F32),
+    ((256, 8192), BF16),
 ]
 
 

time: 54 us -> 51.6 us (0.956)
  Pallas kernels: 50.2 us -> 47.9 us
    pallas_call x1, Pallas kernels: 50.2 us -> 47.9 us  [run(): pl.pallas_call(whole_kernel, name='downward', out_shape=[jax.ShapeDtypeSt...]
where the time goes in v2:
time: 51.6 us; the launch traced here: 51.4 us
  Pallas kernels  47.9 us (93%)
  local copies, waits for them, and re-layouts  2.84 us (6%)
  between operations  0.64 us (1%)
    pallas_call x1, Pallas kernels, run(): pl.pallas_call(whole_kernel, name='downward', out_shape=[jax.ShapeDtypeSt...  47.9 us
    unnamed x2, local copies, waits for them, and re-layouts  2.84 us

profile of v2, /device:TPU:1, one launch (start us, length us, event | category | flops | bytes accessed | tf_op | source)
XLA Modules:
  0.0 51.4 jit_solution(12158223268750923291)
XLA Ops:
  0.6 47.9 %downward.1 = (f32[4,4,768]{2,1,0:T(4,128)}, f32[4,4,768]{2,1,0:T(4,128)}) custom-call(f32[3,4,4,768]{3,2,1,0:T(4,128)} %pos_in.1, f32[4,4,768]{2,1,0:T(4,128)} %chg_in.1, f32[4,4,768]{2,1,0:T(4,128)} %soft_in.1, s32[4,4,12]{2,1,0:T(4,128)} %cnt_in.1, f32[1,1,192]{2,1,0:T(1,128)} %top_in.1, bf16[1,1,192]{2,1,0:T(2,128)(2,1)} %bm_in.1, ...), custom_call_target="tpu_custom_call" | custom-call | flops 10000000000 | bytes 10000000 | tf_op jit(solution)/shard_map/downward/pallas_call | solution.py:694
  48.6 1.4 %copy.14 = f32[4,4,768]{2,1,0:T(4,128)} copy(f32[4,4,768]{2,1,0:T(4,128)} %get-tuple-element.4) | data formatting | bytes 98304
  50.0 1.4 %copy.15 = f32[4,4,768]{2,1,0:T(4,128)} copy(f32[4,4,768]{2,1,0:T(4,128)} %get-tuple-element.5) | data formatting | bytes 98304

commit v3 on v2

--- a/solution.py
+++ b/solution.py
@@ -28,7 +28,7 @@
 
 def unpack_rows(block, base, s2, rows):
     for c in range(32):
-        s2[pl.ds(base * 32 + c, rows, stride=32), :] = block[:, c * 128 : (c + 1) * 128]
+        s2[pl.ds(base * 40 + c, rows, stride=40), :] = block[:, c * 128 : (c + 1) * 128]
 
 
 def pair_rows(first, second, low_lanes):
@@ -72,11 +72,13 @@
         n = (x + ix) * (x + ix) + (y + iy) * (y + iy) + z * z + 0.5 * (s * s)
         feats = [x, x, ix, ix, y, y, iy, iy, z, z, ones, ones, ones] + pieces(n, 3)
         for f in range(16):
-            wt[slot, pl.ds(f, 8, stride=16), :] = feats[f]
-        wt[slot, 128:136, :] = q
+            wt[slot, pl.ds(f, 8, stride=24), :] = feats[f]
+        wt[slot, 192:200, :] = q
     for slot, (_, _, a_mat, q_mat, at) in enumerate(where):
+        tile = [wt[slot + base, zp * 24 : zp * 24 + 16, :] for zp in range(8)]
+        tile = jnp.concatenate(tile + [wt[slot + base, 192:208, :]], axis=0)
         turned = lax.dot_general(
-            same, wt[slot + base].astype(BF16), (((1,), (1,)), ((), ())), preferred_element_type=F32
+            same, tile.astype(BF16), (((1,), (1,)), ((), ())), preferred_element_type=F32
         )
         rows = pl.ds(pl.multiple_of(at * 64, 64), 64)
         a_mat[rows, 0:128] = turned[0:64, 0:128].astype(BF16)
@@ -102,7 +104,7 @@
 
     def put(f, v):
         for zp in range(6):
-            fs[zp, pl.ds(f, 4, stride=16), :] = v[:, zp * 128 : zp * 128 + 128]
+            fs[zp, pl.ds(f, 4, stride=24), :] = v[:, zp * 128 : zp * 128 + 128]
 
     for x in range(4):
         px, py, pz = (pos[d, x] - 0.5 for d in range(3))
@@ -126,7 +128,9 @@
             for f, v in zip((8, 9, 10, 11, 12), [-2.0 * az, -2.0 * bz] + pieces(n, 3)):
                 put(f, v)
             for zp in range(6):
-                made = fs[zp]
+                made = jnp.concatenate(
+                    [fs[zp, y * 24 : y * 24 + 16, :] for y in range(4)], axis=0
+                )
                 if d != 1:
                     made = pltpu.roll(made, 64, 1)
                 for e in range(2):
@@ -472,7 +476,7 @@
     for x in range(4):
         for zp in range(6):
             for f in range(5):
-                ps[pl.ds(x * 192 + f * 8 + 1 + zp, 4, stride=48), :] = own_piece(x, f, zp)
+                ps[pl.ds(x * 224 + f * 8 + 1 + zp, 4, stride=56), :] = own_piece(x, f, zp)
     for zp in range(6):
         for x in range(4):
             mls[pl.ds(x * 32 + zp + 1, 4, stride=8), :] = ms[
@@ -511,7 +515,7 @@
         got = zr[side].astype(F32) * keep
         for x in range(4):
             for f in range(5):
-                ps[pl.ds(x * 192 + f * 8 + zp_l, 4, stride=48), :] = got[
+                ps[pl.ds(x * 224 + f * 8 + zp_l, 4, stride=56), :] = got[
                     f * 16 + x * 4 : f * 16 + x * 4 + 4, :
                 ]
             mls[pl.ds(x * 32 + zp_l, 4, stride=8), :] = got[80 + x * 4 : 84 + x * 4, :]
@@ -540,7 +544,7 @@
     for x in range(4):
         for y in range(4):
             for t in range(3):
-                r = (x * 4 + y) * 48 + t * 16
+                r = (x * 4 + y) * 56 + t * 16
                 pf[1 + x, 1 + y, t] = ps[r : r + 16, :].astype(BF16)
         for yp in range(2):
             r = x * 32 + yp * 16
@@ -566,7 +570,7 @@
         kept = jnp.where(near, 0.0, 1.0).astype(F32)
         tables = []
         for i in range(7):
-            one = s2[pl.ds(pl.multiple_of((g * 7 + i) * 32, 32), 32), :]
+            one = s2[pl.ds(pl.multiple_of((g * 7 + i) * 40, 8), 32), :]
             if 2 <= i <= 4:
                 one = one * kept
             tables.append((one, pltpu.roll(one, 64, 1)))
@@ -625,8 +629,8 @@
     lax.fori_loop(5, 9, own_pairs_y, 0)
     pair_up(48, 0)
     for child in range(4):
-        r = (343 + 2 * child) * 32
-        even, odd = pair_rows(s2[r : r + 32, :], s2[r + 32 : r + 64, :], low_lanes)
+        r = (343 + 2 * child) * 40
+        even, odd = pair_rows(s2[r : r + 32, :], s2[r + 40 : r + 40 + 32, :], low_lanes)
         to = 49 * 384 + child * 64
         t2[to : to + 32, :] = even
         t2[to + 32 : to + 64, :] = odd
@@ -665,8 +669,8 @@
     ((768, 1664), BF16),
     ((6, 9, 256, 256), BF16),
     ((16, 3, 2, 16, 768), BF16),
-    ((6, 64, 128), F32),
-    ((6, 144, 128), F32),
+    ((6, 96, 128), F32),
+    ((6, 208, 128), F32),
     ((16, 2, 8, 768), F32),
 ]
 
@@ -687,9 +691,9 @@
     scratch = [((T2_ROWS, 128), BF16), ((16, 768), F32), ((3, 4, 4, 768), F32)]
     scratch += [((4, 4, 12), jnp.int32), ((1, 1, 192), F32)] + FAR_SCRATCH
     scratch += [(s, BF16) for s in halos]
-    scratch += [((2, 112, 128), BF16), ((2, 112, 128), BF16), ((768, 128), F32), ((128, 128), F32)]
+    scratch += [((2, 112, 128), BF16), ((2, 112, 128), BF16), ((896, 128), F32), ((128, 128), F32)]
     scratch += [((32, 128), F32), ((112, 128), F32), ((224, 128), F32), ((343, 4096), BF16)]
-    scratch += [((352 * 32, 128), F32), ((4, 4, 768), F32), ((4, 4, 768), F32)]
+    scratch += [((352 * 40, 128), F32), ((4, 4, 768), F32), ((4, 4, 768), F32)]
     scratch += [((1, 1, 192), BF16), ((2, 2, 384), BF16), ((4, 4, 768), BF16), ((8, 4096), BF16)]
     return pl.pallas_call(
         whole_kernel,
@@ -712,8 +716,32 @@
     )(*args)
 
 
+def hand_over_kernel(pot_in, loc_in, pot_out, loc_out, sems):
+    copies = [
+        pltpu.make_async_copy(pot_in, pot_out, sems.at[0]),
+        pltpu.make_async_copy(loc_in, loc_out, sems.at[1]),
+    ]
+    for copy in copies:
+        copy.start()
+    for copy in copies:
+        copy.wait()
+
+
+def hand_over(*results):
+    hbm = pl.BlockSpec(memory_space=pltpu.HBM)
+    return pl.pallas_call(
+        hand_over_kernel,
+        name="hand_over",
+        out_shape=[jax.ShapeDtypeStruct((4, 4, 768), F32)] * 2,
+        in_specs=[hbm] * 2,
+        out_specs=[hbm] * 2,
+        scratch_shapes=[pltpu.SemaphoreType.DMA((2,))],
+        compiler_params=pltpu.CompilerParams(vmem_limit_bytes=VMEM_BYTES),
+    )(*results)
+
+
 def per_device(pos, chg, soft, cnt, top, bm, am, lm, m2l, l2l):
-    return tuple(run(pos, chg, soft, cnt, top, bm, am, lm, m2l, l2l))
+    return tuple(hand_over(*run(pos, chg, soft, cnt, top, bm, am, lm, m2l, l2l)))
 
 
 def solution(mesh):

time: 51.6 us -> 49.8 us (0.965)
  local copies, waits for them, and re-layouts: 2.84 us -> 0 us
  Pallas kernels: 47.9 us -> 48.9 us
    pallas_call x0 -> x1, Pallas kernels: none -> 4.1 us  [hand_over(): pl.pallas_call(hand_over_kernel, name='hand_over', out_shape=[jax.ShapeDt...]
    pallas_call x1, Pallas kernels: 47.9 us -> 44.8 us  [run(): pl.pallas_call(whole_kernel, name='downward', out_shape=[jax.ShapeDtypeSt...]
    unnamed x2 -> x0, local copies, waits for them, and re-layouts: 2.84 us -> none
where the time goes in v3:
time: 49.8 us; the launch traced here: 49.6 us
  Pallas kernels  48.9 us (98%)
  between operations  0.64 us (1%)
    pallas_call x1, Pallas kernels, run(): pl.pallas_call(whole_kernel, name='downward', out_shape=[jax.ShapeDtypeSt...  44.8 us
    pallas_call x1, Pallas kernels, hand_over(): pl.pallas_call(hand_over_kernel, name='hand_over', out_shape=[jax.ShapeDt...  4.1 us

profile of v3, /device:TPU:1, one launch (start us, length us, event | category | flops | bytes accessed | tf_op | source)
XLA Modules:
  0.0 49.6 jit_solution(14256666883673058188)
XLA Ops:
  0.6 44.8 %downward.1 = (f32[4,4,768]{2,1,0:T(4,128)}, f32[4,4,768]{2,1,0:T(4,128)}) custom-call(f32[3,4,4,768]{3,2,1,0:T(4,128)} %pos_in.1, f32[4,4,768]{2,1,0:T(4,128)} %chg_in.1, f32[4,4,768]{2,1,0:T(4,128)} %soft_in.1, s32[4,4,12]{2,1,0:T(4,128)} %cnt_in.1, f32[1,1,192]{2,1,0:T(1,128)} %top_in.1, bf16[1,1,192]{2,1,0:T(2,128)(2,1)} %bm_in.1, ...), custom_call_target="tpu_custom_call" | custom-call | flops 10000000000 | bytes 10000000 | tf_op jit(solution)/shard_map/downward/pallas_call | solution.py:698
  45.5 4.1 %hand_over.1 = (f32[4,4,768]{2,1,0:T(4,128)}, f32[4,4,768]{2,1,0:T(4,128)}) custom-call(f32[4,4,768]{2,1,0:T(4,128)} %get-tuple-element.4.pot_in, f32[4,4,768]{2,1,0:T(4,128)} %get-tuple-element.5.loc_in), custom_call_target="tpu_custom_call" | custom-call | tf_op jit(solution)/shard_map/hand_over/pallas_call | solution.py:732

commit v4 on v3

--- a/solution.py
+++ b/solution.py
@@ -716,14 +716,20 @@
     )(*args)
 
 
-def hand_over_kernel(pot_in, loc_in, pot_out, loc_out, sems):
-    copies = [
-        pltpu.make_async_copy(pot_in, pot_out, sems.at[0]),
-        pltpu.make_async_copy(loc_in, loc_out, sems.at[1]),
-    ]
-    for copy in copies:
+def hand_over_kernel(pot_in, loc_in, pot_out, loc_out, held, sems):
+    arrays = ((pot_in, pot_out), (loc_in, loc_out))
+    blocks = [(n, x) for n in range(2) for x in range(4)]
+    came, left = [], []
+    for n, x in blocks:
+        i = n * 4 + x
+        came.append(pltpu.make_async_copy(arrays[n][0].at[x], held.at[n, x], sems.at[0, i]))
+        left.append(pltpu.make_async_copy(held.at[n, x], arrays[n][1].at[x], sems.at[1, i]))
+    for copy in came:
         copy.start()
-    for copy in copies:
+    for first, second in zip(came, left):
+        first.wait()
+        second.start()
+    for copy in left:
         copy.wait()
 
 
@@ -735,7 +741,7 @@
         out_shape=[jax.ShapeDtypeStruct((4, 4, 768), F32)] * 2,
         in_specs=[hbm] * 2,
         out_specs=[hbm] * 2,
-        scratch_shapes=[pltpu.SemaphoreType.DMA((2,))],
+        scratch_shapes=[pltpu.VMEM((2, 4, 4, 768), F32), pltpu.SemaphoreType.DMA((2, 8))],
         compiler_params=pltpu.CompilerParams(vmem_limit_bytes=VMEM_BYTES),
     )(*results)
 

time: 49.8 us -> 47.4 us (0.952)
  Pallas kernels: 48.9 us -> 46.4 us
    pallas_call x1, Pallas kernels: 4.1 us -> 1.56 us  [hand_over(): pl.pallas_call(hand_over_kernel, name='hand_over', out_shape=[jax.ShapeDt...]
where the time goes in v4:
time: 47.4 us; the launch traced here: 47 us
  Pallas kernels  46.4 us (98%)
  between operations  0.64 us (1%)
    pallas_call x1, Pallas kernels, run(): pl.pallas_call(whole_kernel, name='downward', out_shape=[jax.ShapeDtypeSt...  44.8 us
    pallas_call x1, Pallas kernels, hand_over(): pl.pallas_call(hand_over_kernel, name='hand_over', out_shape=[jax.ShapeDt...  1.56 us

profile of v4, /device:TPU:1, one launch (start us, length us, event | category | flops | bytes accessed | tf_op | source)
XLA Modules:
  0.0 47.0 jit_solution(14043959556646818284)
XLA Ops:
  0.6 44.8 %downward.1 = (f32[4,4,768]{2,1,0:T(4,128)}, f32[4,4,768]{2,1,0:T(4,128)}) custom-call(f32[3,4,4,768]{3,2,1,0:T(4,128)} %pos_in.1, f32[4,4,768]{2,1,0:T(4,128)} %chg_in.1, f32[4,4,768]{2,1,0:T(4,128)} %soft_in.1, s32[4,4,12]{2,1,0:T(4,128)} %cnt_in.1, f32[1,1,192]{2,1,0:T(1,128)} %top_in.1, bf16[1,1,192]{2,1,0:T(2,128)(2,1)} %bm_in.1, ...), custom_call_target="tpu_custom_call" | custom-call | flops 10000000000 | bytes 10000000 | tf_op jit(solution)/shard_map/downward/pallas_call | solution.py:698
  45.5 1.6 %hand_over.1 = (f32[4,4,768]{2,1,0:T(4,128)}, f32[4,4,768]{2,1,0:T(4,128)}) custom-call(f32[4,4,768]{2,1,0:T(4,128)} %get-tuple-element.4.pot_in, f32[4,4,768]{2,1,0:T(4,128)} %get-tuple-element.5.loc_in), custom_call_target="tpu_custom_call" | custom-call | tf_op jit(solution)/shard_map/hand_over/pallas_call | solution.py:738

commit v5 on v4

--- a/solution.py
+++ b/solution.py
@@ -376,7 +376,7 @@
         to_lanes[128:256, lanes] = block
         return carry
 
-    lax.fori_loop(0, 64, one, 0)
+    lax.fori_loop(0, 64, one, 0, unroll=4)
 
 
 def whole_kernel(
@@ -502,7 +502,7 @@
         unpack_rows(block, i * 16, s2, 16)
         return carry
 
-    lax.fori_loop(0, 21, unpack, 0)
+    lax.fori_loop(0, 21, unpack, 0, unroll=3)
     unpack_rows(mt[336:343, :].astype(F32), 336, s2, 7)
     unpack_rows(l2l[...].astype(F32), 343, s2, 8)
 
@@ -599,7 +599,7 @@
         pair_some(t - 1)
         return carry
 
-    lax.fori_loop(1, 5, own_columns, 0)
+    lax.fori_loop(1, 5, own_columns, 0, unroll=2)
     lax.fori_loop(1, 5, own_pairs, 0)
     for copy in x_b:
         copy.wait()
@@ -652,7 +652,7 @@
         return carry
 
     lax.fori_loop(0, 2, own_pairs_x, 0)
-    lax.fori_loop(0, 2, last_pairs, 0)
+    lax.fori_loop(0, 2, last_pairs, 0, unroll=True)
     gather_near(near8, near)
     far_kernel(
         gx, gy, gz, ml, ma, mb, t2, near, pos, cnt, top, pot_out, loc_out,

time: 47.4 us -> 46.8 us (0.987)
  Pallas kernels: 46.4 us -> 45.6 us
    pallas_call x1, Pallas kernels: 44.8 us -> 44.1 us  [run(): pl.pallas_call(whole_kernel, name='downward', out_shape=[jax.ShapeDtypeSt...]
where the time goes in v5:
time: 46.8 us; the launch traced here: 46.4 us
  Pallas kernels  45.6 us (97%)
  between operations  0.8 us (2%)
    pallas_call x1, Pallas kernels, run(): pl.pallas_call(whole_kernel, name='downward', out_shape=[jax.ShapeDtypeSt...  44.1 us
    pallas_call x1, Pallas kernels, hand_over(): pl.pallas_call(hand_over_kernel, name='hand_over', out_shape=[jax.ShapeDt...  1.56 us

profile of v5, /device:TPU:1, one launch (start us, length us, event | category | flops | bytes accessed | tf_op | source)
XLA Modules:
  0.0 46.4 jit_solution(12575052472133829709)
XLA Ops:
  0.6 44.1 %downward.1 = (f32[4,4,768]{2,1,0:T(4,128)}, f32[4,4,768]{2,1,0:T(4,128)}) custom-call(f32[3,4,4,768]{3,2,1,0:T(4,128)} %pos_in.1, f32[4,4,768]{2,1,0:T(4,128)} %chg_in.1, f32[4,4,768]{2,1,0:T(4,128)} %soft_in.1, s32[4,4,12]{2,1,0:T(4,128)} %cnt_in.1, f32[1,1,192]{2,1,0:T(1,128)} %top_in.1, bf16[1,1,192]{2,1,0:T(2,128)(2,1)} %bm_in.1, ...), custom_call_target="tpu_custom_call" | custom-call | flops 10000000000 | bytes 10000000 | tf_op jit(solution)/shard_map/downward/pallas_call | solution.py:698
  44.7 1.6 %hand_over.1 = (f32[4,4,768]{2,1,0:T(4,128)}, f32[4,4,768]{2,1,0:T(4,128)}) custom-call(f32[4,4,768]{2,1,0:T(4,128)} %get-tuple-element.4.pot_in, f32[4,4,768]{2,1,0:T(4,128)} %get-tuple-element.5.loc_in), custom_call_target="tpu_custom_call" | custom-call | tf_op jit(solution)/shard_map/hand_over/pallas_call | solution.py:738
